TPU v7x, 512 devices: a whole 4x4x16 slice. The times are simulated.
512 devices in a mesh: gx: 8 (over z_hi, y), yz: 64 (over z_lo, x, core).
Axes of the slice: x: 4, y: 4, z: 16 (z_hi: 2, z_lo: 8; z = z_hi * 8 + z_lo), core: 2. Of those that a mesh axis runs over, the one named last changes fastest.
Arguments:
- adjoint: float32 [12, 64, 1024, 128], P(None, 'gx', 'yz'), may hold values from -6 to 6
- forward: float32 [12, 64, 1024, 128], P(None, 'gx', 'yz'), may hold values from -6 to 6
- coarse_model: float32 [8, 67, 7], P('gx'), may hold values from 0.5 to 1.5
- knot_span: int32 [1024], P('yz'), may hold values from 0 to 63, never falling along the last dimension, each value on 1 to 32 neighbouring positions
- knot_frac: float32 [1024], P('yz'), may hold values from 0 to 1
- dof_cell: int32 [4096], replicated, may hold values from 0 to 65535, as said below
- impedance: float32 [64, 4096], P(None, 'yz'), may hold values from -0.75 to 0.75
- history: float32 [63, 4096], P(None, 'yz'), may hold values from -6 to 6
- plate: bfloat16 [4096, 4096], P('yz'), may hold values from -0.09375 to 0.09375
- coupling: float32 [12, 12], replicated, may hold values from -1.5 to 1.5
- damping: float32 [12], replicated, may hold values from 0.05 to 2
Outputs:
- updated: float32 [12, 64, 1024, 128], P(None, 'gx', 'yz')
- coarse_grad: float32 [8, 67, 7], P('gx')
- reaction: float32 [4096], P('yz')
Inputs may be any that keep to these rules, and one draw needn't show every extreme that they name: `dof_cell`: distinct surface cells.
All inputs are finite; a program needn't handle non-finite values.
Results may differ from a plain program's by a relative error of at most 0.0025.
Values may be sent and summed in bfloat16 or wider, within the bound.
A program may use at most 64 MiB of HBM per device.

v0:
```python
import jax
import jax.numpy as jnp
from jax import lax
from jax.sharding import PartitionSpec as P

HZ = 32


time_step = 0.1
surface_gain = 40.0
grad_norm = 20.0


def extended(cells, sides, width):
    for axis, dim in sides:
        count = lax.axis_size(axis)
        ends = count - 1
        head = lax.slice_in_dim(cells, 0, width, axis=dim)
        tail = lax.slice_in_dim(cells, cells.shape[dim] - width, cells.shape[dim], axis=dim)
        cells = jnp.concatenate(
            [
                lax.ppermute(tail, axis, [(i, (i + 1) % count) for i in range(ends)]),
                cells,
                lax.ppermute(head, axis, [((i + 1) % count, i) for i in range(ends)]),
            ],
            axis=dim,
        )
    return cells


def bspline_weights(param):
    inverse = 1.0 - param
    return (
        inverse**3 / 6.0,
        (3.0 * param**3 - 6.0 * param**2 + 4.0) / 6.0,
        (-3.0 * param**3 + 3.0 * param**2 + 3.0 * param + 1.0) / 6.0,
        param**3 / 6.0,
    )


def basis_rows(span, param, count):
    columns = jnp.arange(count, dtype=jnp.int32)[None, :]
    table = jnp.zeros((span.shape[0], count), jnp.float32)
    for shift_index, weight in enumerate(bspline_weights(param)):
        table = table + jnp.where(columns == span[:, None] + shift_index, weight[:, None], 0.0)
    return table


def depth_rows(depth, count):
    positions = jnp.arange(depth, dtype=jnp.int32)
    span = positions // HZ
    param = (positions.astype(jnp.float32) + 0.5) / HZ - span.astype(jnp.float32)
    return basis_rows(span, param, count)


def on_device(
    adjoint,
    forward,
    coarse_model,
    knot_span,
    knot_frac,
    dof_cell,
    impedance,
    history,
    plate,
    coupling,
    damping,
):
    high = lax.Precision.HIGHEST
    components, cells_x, cells_y, depth = adjoint.shape
    stacked = jnp.concatenate((adjoint, forward), 0)
    padded = extended(stacked, (("gx", 1), ("yz", 2)), 1)
    along_x = padded[:, :, 1:-1]
    along_y = padded[:, 1:-1]
    along_z = jnp.pad(stacked, ((0, 0), (0, 0), (0, 0), (1, 1)))
    laplace = along_x[:, 2:] + along_x[:, :-2] + along_y[:, :, 2:] + along_y[:, :, :-2]
    laplace = laplace + along_z[..., 2:] + along_z[..., :-2] - 6.0 * stacked
    lap_adj = laplace[:components]
    lap_fwd = laplace[components:]
    knots_y = coarse_model.shape[1]
    knots_z = coarse_model.shape[2]
    weights_y = basis_rows(knot_span, knot_frac, knots_y)
    weights_z = depth_rows(depth, knots_z)
    material = jnp.dot(
        jnp.dot(weights_y, coarse_model[0], precision=high), weights_z.T, precision=high
    )
    rows_all = cells_y * lax.axis_size("yz")
    index_x = lax.axis_index("gx") * cells_x + jnp.arange(cells_x, dtype=jnp.int32)
    index_y = lax.axis_index("yz") * cells_y + jnp.arange(cells_y, dtype=jnp.int32)
    cell_ids = (index_x[:, None] * rows_all + index_y[None, :]).reshape(-1)
    selector = (dof_cell[:, None] == cell_ids[None, :]).astype(jnp.float32)
    surface = adjoint[2, :, :, 0].reshape(-1)
    sample_part = jnp.dot(selector, surface, precision=high)
    share_dof = impedance.shape[1]
    summed = lax.psum(sample_part, ("gx", "yz"))
    sample = lax.dynamic_slice_in_dim(summed, lax.axis_index("yz") * share_dof, share_dof, 0)
    impulse = impedance[0] * sample + jnp.sum(impedance[1:] * history, axis=0)
    impulse_half = impulse.astype(jnp.bfloat16)
    plate_part = jnp.dot(
        plate,
        lax.all_gather(impulse_half, "yz", axis=0, tiled=True),
        preferred_element_type=jnp.float32,
    )
    reaction = impulse + plate_part
    reaction_all = lax.all_gather(reaction, "yz", axis=0, tiled=True)
    forcing = jnp.dot(reaction_all, selector, precision=high).reshape(cells_x, cells_y)
    coupled = jnp.einsum("cd,dxyz->cxyz", coupling, lap_adj, precision=high)
    tendency = material[None, None] * (lap_adj + coupled) - damping[:, None, None, None] * adjoint
    updated = adjoint + time_step * tendency
    updated = updated.at[2, :, :, 0].add(time_step * surface_gain * forcing)
    correlation = jnp.sum(jnp.sum(adjoint * lap_fwd, axis=0), axis=0)
    partial_grad = jnp.dot(
        jnp.dot(weights_y.T, correlation, precision=high), weights_z, precision=high
    )
    coarse_grad = lax.psum(partial_grad, "yz")
    coarse_grad = coarse_grad / (grad_norm * (cells_x * cells_y * HZ) ** 0.5)
    return (updated, coarse_grad[None], reaction)


def solution(mesh):
    return jax.shard_map(
        on_device,
        mesh=mesh,
        in_specs=(
            P(None, "gx", "yz", None),
            P(None, "gx", "yz", None),
            P("gx", None, None),
            P("yz"),
            P("yz"),
            P(),
            P(None, "yz"),
            P(None, "yz"),
            P("yz", None),
            P(),
            P(),
        ),
        out_specs=(P(None, "gx", "yz", None), P("gx", None, None), P("yz")),
        check_vma=False,
    )
```

profile of v0, /device:TPU:1, one launch (start us, length us, event | category | flops | bytes accessed | tf_op | source)
XLA Modules:
  0.0 785.4 jit_solution(6059202391087450293)
XLA Ops:
  0.6 0.0 copy-start
  0.7 1.7 copy.23
  2.4 0.5 copy.25
  2.9 0.0 copy-start.8
  2.9 0.0 copy-start.9
  2.9 0.0 copy-start.12
  2.9 0.8 fusion.29
  3.7 1.3 collective-permute-start
  5.0 5.3 collective-permute-start.1
  10.3 0.6 fusion.74
  10.9 0.6 add_multiply_fusion.2
  11.5 0.6 broadcast_add_fusion.2
  12.1 0.1 slice_reduce_fusion
  12.3 0.1 broadcast_add_fusion
  12.4 0.1 add.293
  12.4 0.1 reshape.167
  12.5 2.1 fusion.2
  14.7 117.3 %psum.14 = f32[4096]{0:T(1024)S(1)} all-reduce(f32[4096]{0:T(1024)S(1)} %bitcast.45), channel_id=1, replica_groups=mesh['gx'=8,'yz'=64] {'gx','yz'}, use_global_device_ids=true, to_apply=%region_0.1 | all-reduce | flops 4096 | bytes 32768 | tf_op jit(solution)/shard_map/psum | solution.py:95
  132.0 1.3 dynamic-slice.9
  133.9 0.1 fusion.80
  134.0 0.2 dynamic-update-slice.3
  134.2 212.5 %all-reduce.1 = bf16[4096]{0:T(1024)(128)(2,1)S(1)} all-reduce(bf16[4096]{0:T(1024)(128)(2,1)S(1)} %dynamic-update-slice.3), channel_id=1, replica_groups=mesh['gx'=8,'yz'=64] {'yz'}, use_global_device_ids=true, to_apply=%add.1 | all-reduce | flops 4096 | bytes 16384
  346.7 0.2 fusion.18
  347.0 0.3 dynamic-update-slice.4
  347.2 0.2 fusion.52
  347.4 1.1 fusion.31
  348.5 0.0 collective-permute-done
  348.6 0.8 pad_maximum_fusion.16
  349.4 8.4 %collective-permute-start.2 = (f32[24,10,1,128]{3,0,2,1:T(8,128)S(1)}, f32[24,10,1,128]{3,0,2,1:T(8,128)S(1)}, u32[]{:S(2)}, u32[]{:S(2)}) collective-permute-start(f32[24,10,1,128]{3,0,2,1:T(8,128)S(1)} %get-tuple-element.25), channel_id=1, source_target_pairs={{1,0},{2,1},{3,2},{4,3},{5,4},{6,5},{7,6},{8,7},{9,8},{10,9},{11,1... | collective-permute-start | bytes 368648 | tf_op jit(solution)/shard_map/ppermute | solution.py:24
  357.8 1.9 collective-permute-start.3
  359.7 0.2 pad_maximum_fusion
  359.9 1.7 collective-permute-done.3
  361.6 2.5 fusion.6
  364.1 1.2 copy-done.2
  365.3 0.0 copy-start.7
  365.3 0.0 copy-start.10
  365.4 0.6 fusion.22
  366.0 0.3 fusion.51
  366.4 0.4 fusion.30
  366.7 408.2 %all-reduce.3 = (f32[4096]{0:T(1024)S(1)}, f32[67,7]{0,1:T(8,128)S(1)}) all-reduce(f32[4096]{0:T(1024)S(1)} %dynamic-update-slice.4, f32[67,7]{0,1:T(8,128)S(1)} %fusion.30), channel_id=1, replica_groups=mesh['gx'=8,'yz'=64] {'yz'}, use_global_device_ids=true, to_apply=%add.2 | all-reduce | flops 4565 | bytes 36520
  775.0 1.0 fusion.19
  775.9 0.3 mul.157
  776.2 1.5 fusion.14
  777.7 1.0 copy-done.4
  778.7 0.1 slice_add_fusion
  778.8 3.7 scatter-add.4
  782.5 2.4 copy.28
  784.8 0.6 copy.29
  (44 shorter events, 0.2 us)
Async XLA Ops:
  0.6 346.1 %copy-start = (bf16[64,4096]{1,0:T(8,128)(2,1)S(1)}, bf16[64,4096]{1,0:T(8,128)(2,1)}, u32[]{:S(2)}) copy-start(bf16[64,4096]{1,0:T(8,128)(2,1)} %param.21) | copy-start | bytes 1572868
  0.6 1.7 copy-start.1
  2.9 9.4 %copy-start.8 = (f32[16]{0:T(128)S(1)}, f32[16]{0:T(128)}, u32[]{:S(2)}) copy-start(f32[16]{0:T(128)} %param.17) | copy-start | bytes 196
  2.9 9.4 %copy-start.9 = (s32[16]{0:T(128)S(1)}, s32[16]{0:T(128)}, u32[]{:S(2)}) copy-start(s32[16]{0:T(128)} %param.16) | copy-start | bytes 196
  2.9 129.1 %copy-start.5 = (f32[64,64]{1,0:T(8,128)S(1)}, f32[64,64]{1,0:T(8,128)}, u32[]{:S(2)}) copy-start(f32[64,64]{1,0:T(8,128)} %param.19) | copy-start | bytes 49156
  2.9 129.1 %copy-start.6 = (f32[63,64]{1,0:T(8,128)S(1)}, f32[63,64]{1,0:T(8,128)}, u32[]{:S(2)}) copy-start(f32[63,64]{1,0:T(8,128)} %param.20) | copy-start | bytes 48388
  2.9 344.3 %copy-start.12 = (f32[1,67,7]{1,0,2:T(1,128)S(1)}, f32[1,67,7]{1,0,2:T(1,128)}, u32[]{:S(2)}) copy-start(f32[1,67,7]{1,0,2:T(1,128)} %param.15) | copy-start | bytes 5632
  3.7 344.9 %collective-permute-start = (f32[24,1,16,128]{3,0,2,1:T(8,128)}, f32[24,1,16,128]{3,0,2,1:T(8,128)}, u32[]{:S(2)}, u32[]{:S(2)}) collective-permute-start(f32[24,1,16,128]{3,0,2,1:T(8,128)} %get-tuple-element.28), channel_id=1, source_target_pairs={{64,0},{128,64},{192,128},{256,192},{320,256},{384,320},{448,384},... | collective-permute-start | bytes 589832 | tf_op jit(solution)/shard_map/ppermute | solution.py:24
  5.0 343.6 %collective-permute-start.1 = (f32[24,1,16,128]{3,0,2,1:T(8,128)}, f32[24,1,16,128]{3,0,2,1:T(8,128)}, u32[]{:S(2)}, u32[]{:S(2)}) collective-permute-start(f32[24,1,16,128]{3,0,2,1:T(8,128)} %get-tuple-element.27), channel_id=1, source_target_pairs={{0,64},{64,128},{128,192},{192,256},{256,320},{320,384},{384,448},... | collective-permute-start | bytes 589832 | tf_op jit(solution)/shard_map/ppermute | solution.py:22
  347.0 2.4 copy-start.13
  349.4 10.5 %collective-permute-start.2 = (f32[24,10,1,128]{3,0,2,1:T(8,128)S(1)}, f32[24,10,1,128]{3,0,2,1:T(8,128)S(1)}, u32[]{:S(2)}, u32[]{:S(2)}) collective-permute-start(f32[24,10,1,128]{3,0,2,1:T(8,128)S(1)} %get-tuple-element.25), channel_id=1, source_target_pairs={{1,0},{2,1},{3,2},{4,3},{5,4},{6,5},{7,6},{8,7},{9,8},{10,9},{11,1... | collective-permute-start | bytes 368648 | tf_op jit(solution)/shard_map/ppermute | solution.py:24
  357.8 3.8 collective-permute-start.3
  364.1 1.2 copy-start.2
  365.3 1.0 copy-start.14
  365.3 1.0 copy-start.15
  365.3 1.0 copy-start.16
  365.3 1.0 copy-start.17
  365.3 1.0 copy-start.18
  365.3 1.0 copy-start.19
  365.3 409.6 %copy-start.11 = (s32[4096]{0:T(1024)S(1)}, s32[4096]{0:T(1024)}, u32[]{:S(2)}) copy-start(s32[4096]{0:T(1024)} %param.18) | copy-start | bytes 49156
  365.3 410.9 %copy-start.7 = (f32[12,12]{1,0:T(8,128)S(1)}, f32[12,12]{1,0:T(8,128)}, u32[]{:S(2)}) copy-start(f32[12,12]{1,0:T(8,128)} %param.22) | copy-start | bytes 1732
  365.3 410.9 %copy-start.10 = (f32[12]{0:T(128)S(1)}, f32[12]{0:T(128)}, u32[]{:S(2)}) copy-start(f32[12]{0:T(128)} %param.23) | copy-start | bytes 148
  365.9 410.3 %copy-start.3 = (f32[24,8,16,128]{3,0,2,1:T(8,128)S(1)}, f32[24,8,16,128]{3,0,2,1:T(8,128)}, u32[]{:S(2)}) copy-start(f32[24,8,16,128]{3,0,2,1:T(8,128)} %copy-done.2) | copy-start | bytes 4718596
  777.7 1.0 copy-start.4
where the time goes:
time: 794 us; the launch traced here: 785 us
  blocking collectives  738 us (93%)
  starting transfers between devices  17 us (2%)
  local copies, waits for them, and re-layouts  13.3 us (2%)
    unnamed x2, blocking collectives  621 us
    psum x1, blocking collectives, on_device(): summed = lax.psum(sample_part, ('gx', 'yz'))  117 us
  transfers between devices with their start and end apart: 4, of which 1 were waited for; matrix products, arithmetic and copies ran while one was open for 1% of the time, Pallas kernels for 0%

commit v1 on v0

v1 whole, which is shorter than its diff:
```python
import functools

import jax
import jax.numpy as jnp
from jax import lax
from jax.experimental import pallas as pl
from jax.experimental.pallas import tpu as pltpu
from jax.sharding import PartitionSpec as P

MESH = pl.DeviceIdType.MESH
F32 = jnp.float32
BF16 = jnp.bfloat16
HIGH = lax.Precision.HIGHEST

HZ = 32
time_step = 0.1
surface_gain = 40.0
grad_norm = 20.0

Z_OFFSETS = tuple(sorted(range(-7, 9), key=lambda d: -abs(d)))
NEAR_OFFSETS = tuple(sorted(range(-4, 4), key=lambda d: -abs(d)))
RING_OFFSETS = (2, 1, 3, 0)


def bspline_weights(param):
    inverse = 1.0 - param
    return (
        inverse**3 / 6.0,
        (3.0 * param**3 - 6.0 * param**2 + 4.0) / 6.0,
        (-3.0 * param**3 + 3.0 * param**2 + 3.0 * param + 1.0) / 6.0,
        param**3 / 6.0,
    )


def spread_basis(index, span, param):
    total = 0.0
    for shift, weight in enumerate(bspline_weights(param)):
        total = total + jnp.where(index == span + shift, weight, 0.0)
    return total


def iota(shape, dim):
    return lax.broadcasted_iota(jnp.int32, shape, dim)


def split(values):
    head = values.astype(BF16)
    return head, (values - head.astype(F32)).astype(BF16)


def device_at(z, y, x, c):
    return (lax.div(z, 8) * 4 + y, lax.rem(z, 8) * 8 + x * 2 + c)


def wrap(value, count):
    return lax.rem(value + 2 * count, count)


def kernel(
    adjoint, forward, coarse, span, frac, dof, impedance, history, plate, coupling, damping,
    updated, grad, reaction,
    adj, fwd, upd, plt_buf, cols, surf, taps, taps_all, picked, picked_mate, taps_mate, impulse, one_hot, row_of, react,
    y_out, y_in, corr, x_out, x_in, grad_c, grad_x, grad_z,
    load_sems, send_sems, recv_sems,
):
    gx, yz = lax.axis_index("gx"), lax.axis_index("yz")
    z_hi, y = lax.div(gx, 4), lax.rem(gx, 4)
    z_lo, x, c = lax.div(yz, 8), lax.rem(lax.div(yz, 2), 4), lax.rem(yz, 2)
    z = z_hi * 8 + z_lo
    yx = y * 4 + x
    comps = adj.shape[0]
    has_prev, has_next = gx > 0, gx < 7
    has_left, has_right = yz > 0, yz < 63

    barrier = pltpu.get_barrier_semaphore()

    def greet(device):
        pl.semaphore_signal(barrier, inc=1, device_id=device, device_id_type=MESH)

    greeted = 0
    for d in Z_OFFSETS:
        if abs(d) > 4:
            greet(device_at(wrap(z + d, 16), y, x, c))
            greeted += 1
    for dz in (-4, 4, -3, 3, -2, 2, -1, 1, 0):
        for dx in RING_OFFSETS:
            for dc in (1, 0):
                if (dz, dx, dc) != (0, 0, 0):
                    greet(device_at(wrap(z + dz, 16), y, wrap(x + dx, 4), wrap(c + dc, 2)))
                    greeted += 1
    for dy in (2, 1, 3):
        for dx in RING_OFFSETS:
            greet(device_at(z, wrap(y + dy, 4), wrap(x + dx, 4), c))
            greeted += 1
    jump_up = jnp.logical_and(z_hi == 0, y == 3)
    jump_down = jnp.logical_and(z_hi == 1, y == 0)

    @pl.when(jump_up)
    def _():
        greet((gx + 1, yz))

    @pl.when(jump_down)
    def _():
        greet((gx - 1, yz))

    loads = [
        pltpu.make_async_copy(adjoint.at[2], adj.at[2, pl.ds(1, 8)], load_sems.at[0]),
        pltpu.make_async_copy(adjoint.at[pl.ds(0, 2)], adj.at[pl.ds(0, 2), pl.ds(1, 8)], load_sems.at[1]),
        pltpu.make_async_copy(adjoint.at[pl.ds(3, 9)], adj.at[pl.ds(3, 9), pl.ds(1, 8)], load_sems.at[2]),
        pltpu.make_async_copy(forward, fwd.at[:, pl.ds(1, 8)], load_sems.at[3]),
        pltpu.make_async_copy(plate, plt_buf, load_sems.at[4]),
    ]
    for load in loads:
        load.start()

    tail = jnp.sum(impedance[1:, :] * history[...], axis=0, keepdims=True)
    cols[z, 1:2, :] = jnp.concatenate([impedance[0:1, :], tail], axis=1)
    loads[0].wait()
    surface = adj[2, 1:9].reshape(128, 128)
    cols[z, 0:1, :] = jnp.transpose(surface)[0:1, :]

    pl.semaphore_wait(barrier, greeted + jnp.logical_or(jump_up, jump_down).astype(jnp.int32))

    def remote(src, dst, sem, device):
        return pltpu.make_async_remote_copy(
            src_ref=src, dst_ref=dst, send_sem=send_sems.at[sem], recv_sem=recv_sems.at[sem], device_id=device, device_id_type=MESH
        )

    def arrived(ref, sem):
        pltpu.make_async_copy(ref, ref, recv_sems.at[sem]).wait()

    def sent(ref, sem):
        pltpu.make_async_copy(ref, ref, send_sems.at[sem]).wait()

    for d in Z_OFFSETS:
        if d:
            remote(cols.at[z], cols.at[z], 0, device_at(wrap(z + d, 16), y, x, c)).start()

    for load in loads[1:]:
        load.wait()
    to_prev = remote(adj.at[:, 1], adj.at[:, 9], 1, (lax.max(gx - 1, 0), yz))
    to_next = remote(adj.at[:, 8], adj.at[:, 0], 2, (lax.min(gx + 1, 7), yz))

    @pl.when(has_prev)
    def _():
        to_prev.start()

    @pl.when(has_next)
    def _():
        to_next.start()

    plane = jnp.zeros((16, 128), F32)
    for k in range(comps):
        fwd[k, 0] = plane
        fwd[k, 9] = plane

    @pl.when(gx == 0)
    def _():
        for k in range(comps):
            adj[k, 0] = plane
        x_in[0] = plane

    @pl.when(gx == 7)
    def _():
        for k in range(comps):
            adj[k, 9] = plane
        x_in[1] = plane

    diagonal = iota((16, 16), 0) == iota((16, 16), 1)
    span_col = jnp.sum(jnp.where(diagonal, span[...], 0), axis=1, keepdims=True)
    frac_col = jnp.sum(jnp.where(diagonal, frac[...], 0.0), axis=1, keepdims=True)
    weights_y = spread_basis(iota((16, 128), 1), span_col, frac_col)
    depth = iota((8, 128), 1)
    depth_span = lax.div(depth, HZ)
    weights_z = spread_basis(iota((8, 128), 0), depth_span, (depth.astype(F32) + 0.5) / HZ - depth_span.astype(F32))

    for side, row in ((0, 0), (1, 15)):
        for k in range(comps):
            y_out[side, k] = adj[k, 1:9, row, :]
        y_out[side, comps] = jnp.broadcast_to(weights_y[row : row + 1, :], (8, 128))
    to_left = remote(y_out.at[0], y_in.at[1], 3, (gx, lax.max(yz - 1, 0)))
    to_right = remote(y_out.at[1], y_in.at[0], 4, (gx, lax.min(yz + 1, 63)))

    @pl.when(has_left)
    def _():
        to_left.start()

    @pl.when(has_right)
    def _():
        to_right.start()

    @pl.when(yz == 0)
    def _():
        y_in[0] = jnp.zeros_like(y_in[0])

    @pl.when(yz == 63)
    def _():
        y_in[1] = jnp.zeros_like(y_in[1])

    cell = dof[...]
    cell_x, cell_y = lax.shift_right_logical(cell, 10), lax.bitwise_and(cell, 1023)
    lane = lax.bitwise_and(cell_x, 7) * 16 + lax.bitwise_and(cell_y, 15)
    cell_gx, cell_yz = lax.shift_right_logical(cell_x, 3), lax.shift_right_logical(cell_y, 4)
    cell_row = (
        lax.bitwise_and(cell_gx, 3) * 64
        + lax.bitwise_and(lax.shift_right_logical(cell_yz, 1), 3) * 16
        + lax.shift_right_logical(cell_gx, 2) * 8
        + lax.shift_right_logical(cell_yz, 3)
    )
    row_of[...] = jnp.where(lax.bitwise_and(cell_yz, 1) == c, cell_row, -1)
    for tile in range(16):
        pattern = (iota((128, 256), 0) == lane[:, tile * 256 : tile * 256 + 256]).astype(F32).astype(BF16)
        one_hot[0:128, tile * 256 : tile * 256 + 256] = pattern
        one_hot[128:256, tile * 256 : tile * 256 + 256] = pattern

    cell_rank = iota((128, 1), 0)
    cell_id = (gx * 8 + lax.shift_right_logical(cell_rank, 4)) * 1024 + yz * 16 + lax.bitwise_and(cell_rank, 15)
    found = jnp.zeros((128, 128), F32)
    for tile in range(32):
        label = (iota((1, 128), 1) + (tile * 128 + 1)).astype(F32)
        found = found + jnp.where(cell[:, tile * 128 : tile * 128 + 128] == cell_id, label, 0.0)
    owner = jnp.sum(found, axis=1, keepdims=True).astype(jnp.int32) - 1
    owner_row = lax.shift_right_arithmetic(owner, 6)
    owner_lane = lax.bitwise_and(owner, 127)
    pick_row = (lax.bitwise_and(iota((128, 128), 1), 63) == owner_row).astype(F32).astype(BF16)

    arrived(cols.at[pl.ds(0, 15)], 0)
    surf[yx] = cols[:, 0, :]
    taps_own = cols[0:8, 1, :]
    for k in range(8):
        taps[k, x] = taps_own[k : k + 1, :]
    for dy in RING_OFFSETS:
        for dx in RING_OFFSETS:
            if (dy, dx) != (0, 0):
                remote(surf.at[yx], surf.at[yx], 5, device_at(z, wrap(y + dy, 4), wrap(x + dx, 4), c)).start()
    for dx in (2, 1, 3):
        remote(taps.at[:, x], taps.at[:, x], 6, device_at(z, y, wrap(x + dx, 4), c)).start()

    z_first, z_last = iota((16, 128), 1) == 0, iota((16, 128), 1) == 127
    y_first, y_last = iota((16, 128), 0) == 0, iota((16, 128), 0) == 15

    def laplacian(field, k, i, left, right):
        value = field[k, i]
        total = field[k, i - 1] + field[k, i + 1]
        total = total + jnp.where(z_first, 0.0, pltpu.roll(value, 1, 1)) + jnp.where(z_last, 0.0, pltpu.roll(value, 127, 1))
        total = total + jnp.where(y_first, left, pltpu.roll(value, 1, 0)) + jnp.where(y_last, right, pltpu.roll(value, 15, 0))
        return total - 6.0 * value, value

    def correlate(i, carry):
        for k in range(comps):
            lap, _ = laplacian(fwd, k, i, 0.0, 0.0)
            carry = carry + adj[k, i] * lap
        return carry

    corr[0:16, :] = lax.fori_loop(1, 9, correlate, jnp.zeros((16, 128), F32))

    arrived(taps.at[:, pl.ds(0, 3)], 6)
    for k in range(32):
        taps_all[k : k + 1, :] = taps[k // 4, k % 4]
    mate = (gx, yz + 1 - 2 * c)
    to_mate = remote(taps_all, taps_mate, 7, mate)
    to_mate.start()

    arrived(surf.at[pl.ds(0, 15)], 5)
    head, rest = split(surf[...].reshape(256, 128))
    samples = jnp.concatenate([head, rest], axis=1)
    for tile in range(16):
        lanes = slice(tile * 256, tile * 256 + 256)
        match = jnp.dot(samples, one_hot[:, lanes], preferred_element_type=F32)
        mine = jnp.sum(jnp.where(iota((256, 256), 0) == row_of[:, lanes], match, 0.0), axis=0, keepdims=True)
        picked[2 * tile : 2 * tile + 1, :] = mine[:, 0:128]
        picked[2 * tile + 1 : 2 * tile + 2, :] = mine[:, 128:256]
    picks = remote(picked, picked_mate, 8, mate)
    picks.start()
    to_mate.wait()
    first, second = jnp.where(c == 0, taps_all[...], taps_mate[...]), jnp.where(c == 0, taps_mate[...], taps_all[...])
    low_half = iota((32, 128), 1) < 64
    weight = jnp.where(low_half, first, pltpu.roll(second, 64, 1))
    tails = jnp.where(low_half, pltpu.roll(first, 64, 1), second)
    picks.wait()
    impulse[...] = weight * (picked[...] + picked_mate[...]) + tails

    flat = jnp.concatenate([impulse[k : k + 1, :] for k in range(32)], axis=1).astype(BF16)
    through = lax.dot_general(flat, plt_buf[...], (((1,), (1,)), ((), ())), preferred_element_type=F32)
    through = jnp.concatenate([through, through], axis=1)
    own_half = lax.div(iota((1, 128), 1), 64) == c
    own_row = jnp.where(own_half, through + impulse[pl.ds(lax.div(yz, 2), 1), :], 0.0)
    react[yz] = own_row
    for dz in NEAR_OFFSETS:
        for dx in RING_OFFSETS:
            for dc in (1, 0):
                if (dz, dx, dc) != (0, 0, 0):
                    target = device_at(wrap(z - dz, 16), y, wrap(x + dx, 4), wrap(c + dc, 2))
                    remote(react.at[yz], react.at[yz], 9, target).start()
    reaction[...] = jnp.where(c == 0, own_row[:, 0:64], own_row[:, 64:128])

    @pl.when(has_prev)
    def _():
        arrived(adj.at[:, 0], 2)

    @pl.when(has_next)
    def _():
        arrived(adj.at[:, 9], 1)

    for side, i in ((0, 0), (1, 9)):
        face = jnp.zeros((16, 128), F32)
        for k in range(comps):
            face = face + adj[k, i] * fwd[k, 1 if side == 0 else 8]
        x_out[side] = face
    back_prev = remote(x_out.at[0], x_in.at[1], 10, (lax.max(gx - 1, 0), yz))
    back_next = remote(x_out.at[1], x_in.at[0], 11, (lax.min(gx + 1, 7), yz))

    @pl.when(has_prev)
    def _():
        back_prev.start()

    @pl.when(has_next)
    def _():
        back_next.start()

    @pl.when(has_left)
    def _():
        arrived(y_in.at[0], 4)

    @pl.when(has_right)
    def _():
        arrived(y_in.at[1], 3)

    corr[16:24, :] = jnp.zeros((8, 128), F32)
    for side, row in ((0, 0), (1, 15)):
        edge = jnp.zeros((8, 128), F32)
        for k in range(comps):
            edge = edge + y_in[side, k] * fwd[k, 1:9, row, :]
        corr[16 + side : 17 + side, :] = jnp.sum(edge, axis=0, keepdims=True)

    knots = lax.dot_general(weights_y, coarse[...], (((1,), (1,)), ((), ())), precision=HIGH, preferred_element_type=F32)
    material = time_step * jnp.dot(knots, weights_z, precision=HIGH, preferred_element_type=F32)

    def update(i, _):
        laps = []
        for k in range(comps):
            lap, _ = laplacian(adj, k, i, y_in[0, k, pl.ds(i - 1, 1), :], y_in[1, k, pl.ds(i - 1, 1), :])
            laps.append(lap)
        for k in range(comps):
            mixed = laps[k]
            for m in range(comps):
                mixed = mixed + coupling[k, m] * laps[m]
            value = adj[k, i]
            upd[k, i - 1] = value + material * mixed - (time_step * damping[0, k]) * value
        return 0

    lax.fori_loop(1, 9, update, 0)
    stores = [
        pltpu.make_async_copy(upd.at[pl.ds(0, 2)], updated.at[pl.ds(0, 2)], load_sems.at[5]),
        pltpu.make_async_copy(upd.at[pl.ds(3, 9)], updated.at[pl.ds(3, 9)], load_sems.at[6]),
        pltpu.make_async_copy(upd.at[2], updated.at[2], load_sems.at[7]),
    ]
    stores[0].start()
    stores[1].start()

    arrived(react.at[pl.ds(0, 63)], 9)
    head, rest = split(react[...].reshape(64, 128))
    forces = jnp.dot(pick_row, jnp.concatenate([head, rest], axis=0), preferred_element_type=F32)
    forces = jnp.sum(jnp.where(iota((128, 128), 1) == owner_lane, forces, 0.0), axis=1, keepdims=True)
    forces = (time_step * surface_gain) * forces.reshape(8, 16, 1)
    upd[2] = upd[2] + jnp.where(iota((8, 16, 128), 2) == 0, forces, 0.0)
    stores[2].start()

    @pl.when(has_prev)
    def _():
        arrived(x_in.at[0], 11)

    @pl.when(has_next)
    def _():
        arrived(x_in.at[1], 10)

    corr[0:16, :] = corr[0:16, :] + x_in[0] + x_in[1]
    rows = jnp.concatenate([weights_y, y_in[0, comps, 0:1, :], y_in[1, comps, 0:1, :], jnp.zeros((6, 128), F32)], axis=0)
    part = lax.dot_general(weights_z, corr[...], (((1,), (1,)), ((), ())), precision=HIGH, preferred_element_type=F32)
    grad_c[0] = jnp.dot(part, rows, precision=HIGH, preferred_element_type=F32)
    cores = remote(grad_c.at[0], grad_c.at[1], 12, mate)
    cores.start()
    cores.wait()
    grad_x[x] = grad_c[0] + grad_c[1]
    for dx in (2, 1, 3):
        remote(grad_x.at[x], grad_x.at[x], 13, device_at(z, y, wrap(x + dx, 4), c)).start()
    arrived(grad_x.at[pl.ds(0, 3)], 13)
    grad_z[z_lo] = (grad_x[0] + grad_x[1]) + (grad_x[2] + grad_x[3])
    for d in range(1, 8):
        remote(grad_z.at[z_lo], grad_z.at[z_lo], 14, (gx, lax.rem(z_lo + d, 8) * 8 + x * 2 + c)).start()
    arrived(grad_z.at[pl.ds(0, 7)], 14)
    total = grad_z[0]
    for k in range(1, 8):
        total = total + grad_z[k]
    grad[...] = total / (grad_norm * 4096.0**0.5)

    sent(cols.at[pl.ds(0, 15)], 0)
    sent(surf.at[pl.ds(0, 15)], 5)
    sent(taps.at[:, pl.ds(0, 3)], 6)
    sent(react.at[pl.ds(0, 63)], 9)
    sent(grad_x.at[pl.ds(0, 3)], 13)
    sent(grad_z.at[pl.ds(0, 7)], 14)

    @pl.when(has_prev)
    def _():
        to_prev.wait_send()
        back_prev.wait_send()

    @pl.when(has_next)
    def _():
        to_next.wait_send()
        back_next.wait_send()

    @pl.when(has_left)
    def _():
        to_left.wait_send()

    @pl.when(has_right)
    def _():
        to_right.wait_send()

    for store in stores:
        store.wait()


def on_device(adjoint, forward, coarse_model, knot_span, knot_frac, dof_cell, impedance, history, plate, coupling, damping):
    comps, cells_x, cells_y, depth = adjoint.shape
    knots_y, knots_z = coarse_model.shape[1:]
    coarse = jnp.pad(coarse_model[0].T, ((0, 8 - knots_z), (0, 128 - knots_y)))
    vmem = pl.BlockSpec(memory_space=pltpu.VMEM)
    smem = pl.BlockSpec(memory_space=pltpu.SMEM)
    hbm = pl.BlockSpec(memory_space=pl.ANY)
    updated, grad, reaction = pl.pallas_call(
        kernel,
        out_shape=(
            jax.ShapeDtypeStruct(adjoint.shape, F32),
            jax.ShapeDtypeStruct((8, 128), F32),
            jax.ShapeDtypeStruct((1, 64), F32),
        ),
        in_specs=[hbm, hbm, vmem, vmem, vmem, vmem, vmem, vmem, hbm, smem, smem],
        out_specs=(hbm, vmem, vmem),
        scratch_shapes=[
            pltpu.VMEM((comps, cells_x + 2, cells_y, depth), F32),
            pltpu.VMEM((comps, cells_x + 2, cells_y, depth), F32),
            pltpu.VMEM(adjoint.shape, F32),
            pltpu.VMEM(plate.shape, BF16),
            pltpu.VMEM((16, 2, 128), F32),
            pltpu.VMEM((16, 16, 128), F32),
            pltpu.VMEM((8, 4, 1, 128), F32),
            pltpu.VMEM((32, 128), F32),
            pltpu.VMEM((32, 128), F32),
            pltpu.VMEM((32, 128), F32),
            pltpu.VMEM((32, 128), F32),
            pltpu.VMEM((32, 128), F32),
            pltpu.VMEM((256, 4096), BF16),
            pltpu.VMEM((1, 4096), jnp.int32),
            pltpu.VMEM((64, 1, 128), F32),
            pltpu.VMEM((2, comps + 1, 8, 128), F32),
            pltpu.VMEM((2, comps + 1, 8, 128), F32),
            pltpu.VMEM((24, 128), F32),
            pltpu.VMEM((2, 16, 128), F32),
            pltpu.VMEM((2, 16, 128), F32),
            pltpu.VMEM((2, 8, 128), F32),
            pltpu.VMEM((4, 8, 128), F32),
            pltpu.VMEM((8, 8, 128), F32),
            pltpu.SemaphoreType.DMA((8,)),
            pltpu.SemaphoreType.DMA((15,)),
            pltpu.SemaphoreType.DMA((15,)),
        ],
        compiler_params=pltpu.CompilerParams(collective_id=0, has_side_effects=True, vmem_limit_bytes=40 * 1024 * 1024),
        name="adjoint_step",
    )(
        adjoint, forward, coarse, knot_span.reshape(1, -1), knot_frac.reshape(1, -1), dof_cell.reshape(1, -1),
        impedance, history, plate, coupling, damping.reshape(1, -1),
    )
    return updated, grad[:knots_z, :knots_y].T[None], reaction.reshape(-1)


def solution(mesh):
    return jax.shard_map(
        on_device,
        mesh=mesh,
        in_specs=(
            P(None, "gx", "yz", None),
            P(None, "gx", "yz", None),
            P("gx", None, None),
            P("yz"),
            P("yz"),
            P(),
            P(None, "yz"),
            P(None, "yz"),
            P("yz", None),
            P(),
            P(),
        ),
        out_specs=(P(None, "gx", "yz", None), P("gx", None, None), P("yz")),
        check_vma=False,
    )
```

time: 794 us -> 61.5 us (0.08); the launches traced: 785 us -> 61 us
  blocking collectives: 738 us -> 0 us
  Pallas kernels: 0 us -> 51.5 us
  starting transfers between devices: 17 us -> 0 us
    unnamed x2 -> x0, blocking collectives: 621 us -> none
    psum x1 -> x0, blocking collectives: 117 us -> none  [on_device(): summed = lax.psum(sample_part, ('gx', 'yz'))]
    pallas_call x0 -> x1, Pallas kernels: none -> 51.5 us  [on_device(): pl.pallas_call(kernel, out_shape=(jax.ShapeDtypeStruct(adjoint.shape, F32...]
    ppermute x4 -> x0, starting transfers between devices: 17 us -> none  [the longest x2 9.7 us: extended(): lax.ppermute(head, axis, [((i + 1) % count, i) for i in range(ends)])]
  transfers between devices with their start and end apart: 4 -> 0, of which waited for: 1 -> 0; matrix products, arithmetic and copies ran while one was open for 1% -> 0% of each run, Pallas kernels for 0% -> 0%
where the time goes in v1:
time: 61.5 us; the launch traced here: 61 us
  Pallas kernels  51.5 us (84%)
  local copies, waits for them, and re-layouts  8.81 us (14%)
  between operations  0.69 us (1%)
    pallas_call x1, Pallas kernels, on_device(): pl.pallas_call(kernel, out_shape=(jax.ShapeDtypeStruct(adjoint.shape, F32...  51.5 us
    unnamed x24, local copies, waits for them, and re-layouts  8.8 us

profile of v1, /device:TPU:1, one launch (start us, length us, event | category | flops | bytes accessed | tf_op | source)
XLA Modules:
  0.0 61.0 jit_solution(1344309099402988045)
XLA Ops:
  0.6 0.0 copy-start.5
  0.6 0.0 copy-start.6
  0.7 0.7 %copy.17 = f32[1,67,7]{1,2,0:T(8,128)S(1)} copy(f32[1,67,7]{1,0,2:T(1,128)} %param.13) | data formatting | bytes 3752
  1.3 0.0 copy-start.7
  1.4 0.0 copy-start.8
  1.4 0.0 copy-done.5
  1.4 0.0 copy-done.6
  1.4 0.6 %copy-done.7 = s32[16]{0:T(128)S(1)} copy-done((s32[16]{0:T(128)S(1)}, s32[16]{0:T(128)}, u32[]{:S(2)}) %copy-start.7) | copy-done | bytes 88
  2.0 0.0 copy-done.8
  2.0 0.0 copy-start
  2.0 1.1 %copy-done = f32[12,8,16,128]{3,2,1,0:T(8,128)S(1)} copy-done((f32[12,8,16,128]{3,2,1,0:T(8,128)S(1)}, f32[12,8,16,128]{3,2,1,0:T(8,128)}, u32[]{:S(2)}) %copy-start) | copy-done | bytes 786456
  3.2 0.0 copy-start.1
  3.2 1.1 %copy-done.1 = f32[12,8,16,128]{3,2,1,0:T(8,128)S(1)} copy-done((f32[12,8,16,128]{3,2,1,0:T(8,128)S(1)}, f32[12,8,16,128]{3,2,1,0:T(8,128)}, u32[]{:S(2)}) %copy-start.1) | copy-done | bytes 786456
  4.3 0.0 copy-start.2
  4.3 1.0 %copy-done.2 = bf16[64,4096]{1,0:T(8,128)(2,1)S(1)} copy-done((bf16[64,4096]{1,0:T(8,128)(2,1)S(1)}, bf16[64,4096]{1,0:T(8,128)(2,1)}, u32[]{:S(2)}) %copy-start.2) | copy-done | bytes 524312
  5.3 0.0 copy-start.3
  5.3 0.8 %copy-done.3 = f32[64,64]{1,0:T(8,128)S(1)} copy-done((f32[64,64]{1,0:T(8,128)S(1)}, f32[64,64]{1,0:T(8,128)}, u32[]{:S(2)}) %copy-start.3) | copy-done | bytes 16408
  6.1 0.0 copy-start.4
  6.1 0.8 %copy-done.4 = f32[63,64]{1,0:T(8,128)S(1)} copy-done((f32[63,64]{1,0:T(8,128)S(1)}, f32[63,64]{1,0:T(8,128)}, u32[]{:S(2)}) %copy-start.4) | copy-done | bytes 16152
  6.8 0.0 copy-start.9
  6.8 0.7 %copy-done.9 = f32[12]{0:T(128)S(1)} copy-done((f32[12]{0:T(128)S(1)}, f32[12]{0:T(128)}, u32[]{:S(2)}) %copy-start.9) | copy-done | bytes 72
  7.5 51.5 %adjoint_step.1 = (f32[12,8,16,128]{3,2,1,0:T(8,128)S(1)}, f32[8,128]{1,0:T(8,128)S(1)}, f32[1,64]{1,0:T(1,128)S(1)}) custom-call(f32[12,8,16,128]{3,2,1,0:T(8,128)S(1)} %copy-done, f32[12,8,16,128]{3,2,1,0:T(8,128)S(1)} %copy-done.1, f32[8,128]{1,0:T(8,128)S(1)} %pad.4.coarse, s32[1,16]{1,0:T(1,128)S(1)} %bitcast.15, f32[1,16]{1,0:T(1,128)S(1)} %bitcast.16, ...), custom_call_target="tpu_custom_call" | custom-call | tf_op jit(solution)/shard_map/adjoint_step/pallas_call | solution.py:433
  59.0 0.6 copy.14
  59.6 0.9 %copy.20 = f32[12,8,16,128]{3,2,1,0:T(8,128)} copy(f32[12,8,16,128]{3,2,1,0:T(8,128)S(1)} %get-tuple-element.15) | data formatting | bytes 1572864
  60.5 0.5 copy.21
  (2 shorter events, 0.0 us)
Async XLA Ops:
  0.6 0.7 %copy-start.5 = (s32[4096]{0:T(1024)S(1)}, s32[4096]{0:T(1024)}, u32[]{:S(2)}) copy-start(s32[4096]{0:T(1024)} %param.16) | copy-start | bytes 49156
  0.6 0.7 %copy-start.6 = (f32[12,12]{1,0:T(8,128)S(1)}, f32[12,12]{1,0:T(8,128)}, u32[]{:S(2)}) copy-start(f32[12,12]{1,0:T(8,128)} %coupling.1) | copy-start | bytes 1732
  1.3 0.7 %copy-start.7 = (s32[16]{0:T(128)S(1)}, s32[16]{0:T(128)}, u32[]{:S(2)}) copy-start(s32[16]{0:T(128)} %param.14) | copy-start | bytes 196
  1.4 0.7 %copy-start.8 = (f32[16]{0:T(128)S(1)}, f32[16]{0:T(128)}, u32[]{:S(2)}) copy-start(f32[16]{0:T(128)} %param.15) | copy-start | bytes 196
  2.0 1.1 %copy-start = (f32[12,8,16,128]{3,2,1,0:T(8,128)S(1)}, f32[12,8,16,128]{3,2,1,0:T(8,128)}, u32[]{:S(2)}) copy-start(f32[12,8,16,128]{3,2,1,0:T(8,128)} %adjoint.1) | copy-start | bytes 2359300
  3.2 1.1 %copy-start.1 = (f32[12,8,16,128]{3,2,1,0:T(8,128)S(1)}, f32[12,8,16,128]{3,2,1,0:T(8,128)}, u32[]{:S(2)}) copy-start(f32[12,8,16,128]{3,2,1,0:T(8,128)} %forward.1) | copy-start | bytes 2359300
  4.3 1.0 %copy-start.2 = (bf16[64,4096]{1,0:T(8,128)(2,1)S(1)}, bf16[64,4096]{1,0:T(8,128)(2,1)}, u32[]{:S(2)}) copy-start(bf16[64,4096]{1,0:T(8,128)(2,1)} %plate.1) | copy-start | bytes 1572868
  5.3 0.8 %copy-start.3 = (f32[64,64]{1,0:T(8,128)S(1)}, f32[64,64]{1,0:T(8,128)}, u32[]{:S(2)}) copy-start(f32[64,64]{1,0:T(8,128)} %impedance.1) | copy-start | bytes 49156
  6.1 0.8 %copy-start.4 = (f32[63,64]{1,0:T(8,128)S(1)}, f32[63,64]{1,0:T(8,128)}, u32[]{:S(2)}) copy-start(f32[63,64]{1,0:T(8,128)} %history.1) | copy-start | bytes 48388
  6.8 0.7 %copy-start.9 = (f32[12]{0:T(128)S(1)}, f32[12]{0:T(128)}, u32[]{:S(2)}) copy-start(f32[12]{0:T(128)} %param.21) | copy-start | bytes 148

commit v2 on v1

v2 whole, which is shorter than its diff:
```python
import functools

import jax
import jax.numpy as jnp
from jax import lax
from jax.experimental import pallas as pl
from jax.experimental.pallas import tpu as pltpu
from jax.sharding import PartitionSpec as P

MESH = pl.DeviceIdType.MESH
F32 = jnp.float32
BF16 = jnp.bfloat16
HIGH = lax.Precision.HIGHEST

HZ = 32
VMEM_BYTES = 16 * 1024 * 1024
time_step = 0.1
surface_gain = 40.0
grad_norm = 20.0

NEAR_OFFSETS = tuple(sorted(range(-4, 4), key=lambda d: -abs(d)))
RING_OFFSETS = (2, 1, 3, 0)


def bspline_weights(param):
    inverse = 1.0 - param
    return (
        inverse**3 / 6.0,
        (3.0 * param**3 - 6.0 * param**2 + 4.0) / 6.0,
        (-3.0 * param**3 + 3.0 * param**2 + 3.0 * param + 1.0) / 6.0,
        param**3 / 6.0,
    )


def spread_basis(index, span, param):
    total = 0.0
    for shift, weight in enumerate(bspline_weights(param)):
        total = total + jnp.where(index == span + shift, weight, 0.0)
    return total


def iota(shape, dim):
    return lax.broadcasted_iota(jnp.int32, shape, dim)


def split(values):
    head = values.astype(BF16)
    return head, (values - head.astype(F32)).astype(BF16)


def device_at(z, y, x, c):
    return (lax.div(z, 8) * 4 + y, lax.rem(z, 8) * 8 + x * 2 + c)


def wrap(value, count):
    return lax.rem(value + 2 * count, count)


def kernel(
    adjoint, forward, coarse_hbm, span_hbm, frac_hbm, dof_hbm, impedance_hbm, history_hbm, plate, coupling_hbm, damping_hbm,
    updated, grad, reaction,
    coarse, span, frac, dof, impedance, history, coupling, damping,
    adj, fwd, plt_buf, cols, surf, taps, taps_all, picked, picked_mate, taps_mate, impulse, one_hot, row_of, react,
    y_out, y_in, corr, x_out, x_in, grad_c, grad_x, grad_z, face_adj, face_fwd, face_weights, weights_out,
    load_sems, send_sems, recv_sems, credit,
):
    gx, yz = lax.axis_index("gx"), lax.axis_index("yz")
    z_hi, y = lax.div(gx, 4), lax.rem(gx, 4)
    z_lo, x, c = lax.div(yz, 8), lax.rem(lax.div(yz, 2), 4), lax.rem(yz, 2)
    z = z_hi * 8 + z_lo
    yx = y * 4 + x
    comps = adj.shape[0]
    has_prev, has_next = gx > 0, gx < 7
    has_left, has_right = yz > 0, yz < 63
    mate = (gx, yz + 1 - 2 * c)

    upper, lower = jnp.logical_and(z_hi == 0, y == 3), jnp.logical_and(z_hi == 1, y == 0)
    jump = jnp.logical_or(upper, lower)
    near_prev, near_next = jnp.logical_and(has_prev, jnp.logical_not(lower)), jnp.logical_and(has_next, jnp.logical_not(upper))
    z_half = lax.rem(z_lo + 4, 8)
    half_way = device_at(z_hi * 8 + z_half, y, x, c)
    across = device_at((1 - z_hi) * 8 + z_half, 3 - y, x, c)

    barrier = pltpu.get_barrier_semaphore()

    def greet(device):
        pl.semaphore_signal(barrier, inc=1, device_id=device, device_id_type=MESH)

    greeted = 24 + has_left.astype(jnp.int32) + has_right.astype(jnp.int32) + jump.astype(jnp.int32)

    @pl.when(jump)
    def _():
        greet(across)

    for d in (4, -4, 3, -3, 2, -2, 1, -1):
        greet(device_at(wrap(z + d, 16), y, x, c))
    for dy in RING_OFFSETS:
        for dx in RING_OFFSETS:
            if (dy, dx) != (0, 0):
                greet(device_at(z, wrap(y + dy, 4), wrap(x + dx, 4), c))
    greet(mate)

    @pl.when(has_left)
    def _():
        greet((gx, yz - 1))

    @pl.when(has_right)
    def _():
        greet((gx, yz + 1))

    loads = [
        pltpu.make_async_copy(adjoint.at[2], adj.at[2, pl.ds(1, 8)], load_sems.at[0]),
        pltpu.make_async_copy(impedance_hbm, impedance, load_sems.at[8]),
        pltpu.make_async_copy(history_hbm, history, load_sems.at[9]),
        pltpu.make_async_copy(adjoint.at[pl.ds(0, 2)], adj.at[pl.ds(0, 2), pl.ds(1, 8)], load_sems.at[1]),
        pltpu.make_async_copy(adjoint.at[pl.ds(3, 9)], adj.at[pl.ds(3, 9), pl.ds(1, 8)], load_sems.at[2]),
        pltpu.make_async_copy(forward, fwd.at[:, pl.ds(1, 8)], load_sems.at[3]),
        pltpu.make_async_copy(plate, plt_buf, load_sems.at[4]),
        pltpu.make_async_copy(coarse_hbm, coarse, load_sems.at[10]),
        pltpu.make_async_copy(span_hbm, span, load_sems.at[11]),
        pltpu.make_async_copy(frac_hbm, frac, load_sems.at[12]),
        pltpu.make_async_copy(dof_hbm, dof, load_sems.at[13]),
        pltpu.make_async_copy(coupling_hbm, coupling, load_sems.at[14]),
        pltpu.make_async_copy(damping_hbm, damping, load_sems.at[15]),
    ]
    for load in loads:
        load.start()

    loads[1].wait()
    loads[2].wait()
    tail = jnp.sum(impedance[1:, :] * history[...], axis=0, keepdims=True)
    cols[z, 1:2, :] = jnp.concatenate([impedance[0:1, :], tail], axis=1)
    loads[0].wait()
    surface = adj[2, 1:9].reshape(128, 128)
    cols[z, 0:1, :] = jnp.transpose(surface)[0:1, :]

    pl.semaphore_wait(barrier, greeted)

    def remote(src, dst, sem, device):
        return pltpu.make_async_remote_copy(
            src_ref=src, dst_ref=dst, send_sem=send_sems.at[sem], recv_sem=recv_sems.at[sem], device_id=device, device_id_type=MESH
        )

    def arrived(ref, sem):
        pltpu.make_async_copy(ref, ref, recv_sems.at[sem]).wait()

    def sent(ref, sem):
        pltpu.make_async_copy(ref, ref, send_sems.at[sem]).wait()

    for d in (4, -4, 3, -3, 2, -2, 1, -1):
        remote(cols.at[z], cols.at[z], 0, device_at(wrap(z + d, 16), y, x, c)).start()

    @pl.when(jump)
    def _():
        pl.semaphore_signal(credit, inc=1, device_id=across, device_id_type=MESH)

    for load in loads[3:]:
        load.wait()
    to_prev = remote(adj.at[:, 1], adj.at[:, 9], 1, (lax.max(gx - 1, 0), yz))
    to_next = remote(adj.at[:, 8], adj.at[:, 0], 2, (lax.min(gx + 1, 7), yz))

    @pl.when(near_prev)
    def _():
        to_prev.start()

    @pl.when(near_next)
    def _():
        to_next.start()

    plane = jnp.zeros((16, 128), F32)
    for k in range(comps):
        fwd[k, 0] = plane
        fwd[k, 9] = plane

    @pl.when(gx == 0)
    def _():
        for k in range(comps):
            adj[k, 0] = plane

    @pl.when(gx == 7)
    def _():
        for k in range(comps):
            adj[k, 9] = plane

    @pl.when(jnp.logical_not(near_prev))
    def _():
        x_in[0] = plane

    @pl.when(jnp.logical_not(near_next))
    def _():
        x_in[1] = plane

    diagonal = iota((16, 16), 0) == iota((16, 16), 1)
    span_col = jnp.sum(jnp.where(diagonal, span[...], 0), axis=1, keepdims=True)
    frac_col = jnp.sum(jnp.where(diagonal, frac[...], 0.0), axis=1, keepdims=True)
    weights_y = spread_basis(iota((16, 128), 1), span_col, frac_col)
    depth = iota((8, 128), 1)
    depth_span = lax.div(depth, HZ)
    weights_z = spread_basis(iota((8, 128), 0), depth_span, (depth.astype(F32) + 0.5) / HZ - depth_span.astype(F32))

    weights_out[...] = weights_y
    for side, row in ((0, 0), (1, 15)):
        for k in range(comps):
            y_out[side, k] = adj[k, 1:9, row, :]
        y_out[side, comps] = jnp.broadcast_to(weights_y[row : row + 1, :], (8, 128))
    to_left = remote(y_out.at[0], y_in.at[1], 3, (gx, lax.max(yz - 1, 0)))
    to_right = remote(y_out.at[1], y_in.at[0], 4, (gx, lax.min(yz + 1, 63)))

    @pl.when(has_left)
    def _():
        to_left.start()

    @pl.when(has_right)
    def _():
        to_right.start()

    face = jnp.where(upper, 8, 1)
    face_copies = (
        remote(adj.at[:, face], face_adj, 15, half_way),
        remote(fwd.at[:, face], face_fwd, 16, across),
        remote(weights_out, face_weights, 17, half_way),
    )

    @pl.when(jump)
    def _():
        for copy in face_copies:
            copy.start()

    @pl.when(yz == 0)
    def _():
        y_in[0] = jnp.zeros_like(y_in[0])

    @pl.when(yz == 63)
    def _():
        y_in[1] = jnp.zeros_like(y_in[1])

    cell = dof[...]
    cell_x, cell_y = lax.shift_right_logical(cell, 10), lax.bitwise_and(cell, 1023)
    lane = lax.bitwise_and(cell_x, 7) * 16 + lax.bitwise_and(cell_y, 15)
    cell_gx, cell_yz = lax.shift_right_logical(cell_x, 3), lax.shift_right_logical(cell_y, 4)
    cell_row = (
        lax.bitwise_and(cell_gx, 3) * 64
        + lax.bitwise_and(lax.shift_right_logical(cell_yz, 1), 3) * 16
        + lax.shift_right_logical(cell_gx, 2) * 8
        + lax.shift_right_logical(cell_yz, 3)
    )
    row_of[...] = jnp.where(lax.bitwise_and(cell_yz, 1) == c, cell_row, -1)
    for tile in range(16):
        pattern = (iota((128, 256), 0) == lane[:, tile * 256 : tile * 256 + 256]).astype(F32).astype(BF16)
        one_hot[0:128, tile * 256 : tile * 256 + 256] = pattern
        one_hot[128:256, tile * 256 : tile * 256 + 256] = pattern

    cell_rank = iota((128, 1), 0)
    cell_id = (gx * 8 + lax.shift_right_logical(cell_rank, 4)) * 1024 + yz * 16 + lax.bitwise_and(cell_rank, 15)
    found = jnp.zeros((128, 128), F32)
    for tile in range(32):
        label = (iota((1, 128), 1) + (tile * 128 + 1)).astype(F32)
        found = found + jnp.where(cell[:, tile * 128 : tile * 128 + 128] == cell_id, label, 0.0)
    owner = jnp.sum(found, axis=1, keepdims=True).astype(jnp.int32) - 1
    owner_row = lax.shift_right_arithmetic(owner, 6)
    owner_lane = lax.bitwise_and(owner, 127)
    pick_row = (lax.bitwise_and(iota((128, 128), 1), 63) == owner_row).astype(F32).astype(BF16)

    arrived(cols.at[pl.ds(0, 8)], 0)
    for d in (4, 3, 2, 1):
        slot = wrap(z + d, 16)
        remote(cols.at[slot], cols.at[slot], 18, device_at(wrap(z - 4, 16), y, x, c)).start()
    for d in (-3, -2, -1):
        slot = wrap(z + d, 16)
        remote(cols.at[slot], cols.at[slot], 18, device_at(wrap(z + 4, 16), y, x, c)).start()

    @pl.when(jump)
    def _():
        pl.semaphore_wait(credit, 1)

    @pl.when(lower)
    def _():
        to_prev.start()

    @pl.when(upper)
    def _():
        to_next.start()

    z_first, z_last = iota((16, 128), 1) == 0, iota((16, 128), 1) == 127
    y_first, y_last = iota((16, 128), 0) == 0, iota((16, 128), 0) == 15

    def laplacian(field, k, i, left, right):
        value = field[k, i]
        total = field[k, i - 1] + field[k, i + 1]
        total = total + jnp.where(z_first, 0.0, pltpu.roll(value, 1, 1)) + jnp.where(z_last, 0.0, pltpu.roll(value, 127, 1))
        total = total + jnp.where(y_first, left, pltpu.roll(value, 1, 0)) + jnp.where(y_last, right, pltpu.roll(value, 15, 0))
        return total - 6.0 * value, value

    def correlate(i, carry):
        for k in range(comps):
            lap, _ = laplacian(fwd, k, i, 0.0, 0.0)
            carry = carry + adj[k, i] * lap
        return carry

    corr[0:16, :] = lax.fori_loop(1, 9, correlate, jnp.zeros((16, 128), F32))

    back_prev = remote(x_out.at[0], x_in.at[1], 10, (lax.max(gx - 1, 0), yz))
    back_next = remote(x_out.at[1], x_in.at[0], 11, (lax.min(gx + 1, 7), yz))

    def send_back(side, halo, sem, inner, copy):
        arrived(adj.at[:, halo], sem)
        product = plane
        for k in range(comps):
            product = product + adj[k, halo] * fwd[k, inner]
        x_out[side] = product
        copy.start()

    @pl.when(near_prev)
    def _():
        send_back(0, 0, 2, 1, back_prev)

    @pl.when(near_next)
    def _():
        send_back(1, 9, 1, 8, back_next)

    arrived(cols.at[pl.ds(0, 7)], 18)
    surf[yx] = cols[:, 0, :]
    taps_own = cols[0:8, 1, :]
    for k in range(8):
        taps[k, x] = taps_own[k : k + 1, :]
    for dy in RING_OFFSETS:
        for dx in RING_OFFSETS:
            if (dy, dx) != (0, 0):
                remote(surf.at[yx], surf.at[yx], 5, device_at(z, wrap(y + dy, 4), wrap(x + dx, 4), c)).start()
    for dx in (2, 1, 3):
        remote(taps.at[:, x], taps.at[:, x], 6, device_at(z, y, wrap(x + dx, 4), c)).start()

    @pl.when(has_left)
    def _():
        arrived(y_in.at[0], 4)

    @pl.when(has_right)
    def _():
        arrived(y_in.at[1], 3)

    corr[16:24, :] = jnp.zeros((8, 128), F32)
    for side, row in ((0, 0), (1, 15)):
        edge = jnp.zeros((8, 128), F32)
        for k in range(comps):
            edge = edge + y_in[side, k] * fwd[k, 1:9, row, :]
        corr[16 + side : 17 + side, :] = jnp.sum(edge, axis=0, keepdims=True)

    knots_z, _, knots_y = coarse.shape
    material = jnp.zeros((16, 128), F32)
    for k in range(knots_z):
        knot = jnp.sum(weights_y[:, 0:knots_y] * coarse[k], axis=1, keepdims=True)
        material = material + knot * weights_z[k : k + 1, :]
    material = time_step * material

    def update(i):
        laps = []
        for k in range(comps):
            lap, _ = laplacian(adj, k, i, y_in[0, k, pl.ds(i - 1, 1), :], y_in[1, k, pl.ds(i - 1, 1), :])
            laps.append(lap)
        for k in range(comps):
            mixed = laps[k]
            for m in range(comps):
                mixed = mixed + coupling[k, m] * laps[m]
            value = adj[k, i]
            updated[k, i - 1] = value + material * mixed - (time_step * damping[0, k]) * value

    @pl.loop(2, 8)
    def _(i):
        update(i)

    arrived(taps.at[:, pl.ds(0, 3)], 6)
    for k in range(32):
        taps_all[k : k + 1, :] = taps[k // 4, k % 4]
    to_mate = remote(taps_all, taps_mate, 7, mate)
    to_mate.start()

    arrived(surf.at[pl.ds(0, 15)], 5)
    head, rest = split(surf[...].reshape(256, 128))
    samples = jnp.concatenate([head, rest], axis=1)
    for tile in range(16):
        lanes = slice(tile * 256, tile * 256 + 256)
        match = jnp.dot(samples, one_hot[:, lanes], preferred_element_type=F32)
        mine = jnp.sum(jnp.where(iota((256, 256), 0) == row_of[:, lanes], match, 0.0), axis=0, keepdims=True)
        picked[2 * tile : 2 * tile + 1, :] = mine[:, 0:128]
        picked[2 * tile + 1 : 2 * tile + 2, :] = mine[:, 128:256]
    picks = remote(picked, picked_mate, 8, mate)
    picks.start()

    @pl.when(near_prev)
    def _():
        arrived(x_in.at[0], 11)

    @pl.when(near_next)
    def _():
        arrived(x_in.at[1], 10)

    def project(cells, rows):
        part = lax.dot_general(weights_z, cells, (((1,), (1,)), ((), ())), precision=HIGH, preferred_element_type=F32)
        return jnp.dot(part, rows, precision=HIGH, preferred_element_type=F32)

    corr[0:16, :] = corr[0:16, :] + x_in[0] + x_in[1]
    rows = jnp.concatenate([weights_y, y_in[0, comps, 0:1, :], y_in[1, comps, 0:1, :], jnp.zeros((6, 128), F32)], axis=0)
    grad_c[0] = project(corr[...], rows)

    @pl.when(jump)
    def _():
        arrived(face_adj, 15)
        arrived(face_fwd, 16)
        arrived(face_weights, 17)
        product = plane
        for k in range(comps):
            product = product + face_adj[k] * face_fwd[k]
        grad_c[0] = grad_c[0] + project(product, face_weights[...])

    cores = remote(grad_c.at[0], grad_c.at[1], 12, mate)
    cores.start()

    to_mate.wait()
    first, second = jnp.where(c == 0, taps_all[...], taps_mate[...]), jnp.where(c == 0, taps_mate[...], taps_all[...])
    low_half = iota((32, 128), 1) < 64
    weight = jnp.where(low_half, first, pltpu.roll(second, 64, 1))
    tails = jnp.where(low_half, pltpu.roll(first, 64, 1), second)
    picks.wait()
    impulse[...] = weight * (picked[...] + picked_mate[...]) + tails

    flat = jnp.concatenate([impulse[k : k + 1, :] for k in range(32)], axis=1).astype(BF16)
    through = lax.dot_general(flat, plt_buf[...], (((1,), (1,)), ((), ())), preferred_element_type=F32)
    through = jnp.concatenate([through, through], axis=1)
    own_half = lax.div(iota((1, 128), 1), 64) == c
    own_row = jnp.where(own_half, through + impulse[pl.ds(lax.div(yz, 2), 1), :], 0.0)
    react[yz] = own_row
    for dz in NEAR_OFFSETS:
        for dx in RING_OFFSETS:
            for dc in (1, 0):
                if (dz, dx, dc) != (0, 0, 0):
                    target = device_at(wrap(z - dz, 16), y, wrap(x + dx, 4), wrap(c + dc, 2))
                    remote(react.at[yz], react.at[yz], 9, target).start()
    reaction[...] = jnp.where(c == 0, own_row[:, 0:64], own_row[:, 64:128])

    cores.wait()
    grad_x[x] = grad_c[0] + grad_c[1]
    for dx in (2, 1, 3):
        remote(grad_x.at[x], grad_x.at[x], 13, device_at(z, y, wrap(x + dx, 4), c)).start()
    arrived(grad_x.at[pl.ds(0, 3)], 13)
    grad_z[z_lo] = (grad_x[0] + grad_x[1]) + (grad_x[2] + grad_x[3])
    for d in (7, 6, 5, 4, 3, 2, 1):
        remote(grad_z.at[z_lo], grad_z.at[z_lo], 14, (gx, lax.rem(z_lo + d, 8) * 8 + x * 2 + c)).start()

    @pl.when(lower)
    def _():
        arrived(adj.at[:, 0], 2)

    @pl.when(upper)
    def _():
        arrived(adj.at[:, 9], 1)

    @pl.loop(0, 2)
    def _(side):
        update(1 + 7 * side)

    arrived(react.at[pl.ds(0, 63)], 9)
    head, rest = split(react[...].reshape(64, 128))
    forces = jnp.dot(pick_row, jnp.concatenate([head, rest], axis=0), preferred_element_type=F32)
    forces = jnp.sum(jnp.where(iota((128, 128), 1) == owner_lane, forces, 0.0), axis=1, keepdims=True)
    forces = (time_step * surface_gain) * forces.reshape(8, 16, 1)
    updated[2] = updated[2] + jnp.where(iota((8, 16, 128), 2) == 0, forces, 0.0)

    arrived(grad_z.at[pl.ds(0, 7)], 14)
    total = grad_z[0]
    for k in range(1, 8):
        total = total + grad_z[k]
    total = total / (grad_norm * 4096.0**0.5)
    for k in range(knots_z):
        grad[k] = total[k : k + 1, 0:knots_y]

    sent(cols.at[pl.ds(0, 8)], 0)
    sent(cols.at[pl.ds(0, 7)], 18)
    sent(surf.at[pl.ds(0, 15)], 5)
    sent(taps.at[:, pl.ds(0, 3)], 6)
    sent(react.at[pl.ds(0, 63)], 9)
    sent(grad_x.at[pl.ds(0, 3)], 13)
    sent(grad_z.at[pl.ds(0, 7)], 14)
    for present, copy in (
        (has_prev, to_prev), (has_next, to_next), (has_left, to_left), (has_right, to_right),
        (near_prev, back_prev), (near_next, back_next),
        (jump, face_copies[0]), (jump, face_copies[1]), (jump, face_copies[2]),
    ):
        pl.when(present)(copy.wait_send)


def store_results(*refs):
    count = len(refs) // 2
    copies = [pltpu.make_async_copy(refs[k], refs[count + k], refs[-1].at[k]) for k in range(count)]
    for copy in copies:
        copy.start()
    for copy in copies:
        copy.wait()


def on_device(adjoint, forward, coarse_model, knot_span, knot_frac, dof_cell, impedance, history, plate, coupling, damping):
    comps, cells_x, cells_y, depth = adjoint.shape
    knots_y, knots_z = coarse_model.shape[1:]
    vmem = pl.BlockSpec(memory_space=pltpu.VMEM)
    hbm = pl.BlockSpec(memory_space=pltpu.HBM)
    anywhere = pl.BlockSpec(memory_space=pl.ANY)
    updated, grad, reaction = pl.pallas_call(
        kernel,
        out_shape=(
            jax.ShapeDtypeStruct(adjoint.shape, F32),
            jax.ShapeDtypeStruct((knots_z, 1, knots_y), F32),
            jax.ShapeDtypeStruct((1, 64), F32),
        ),
        in_specs=[hbm] * 11,
        out_specs=(vmem, vmem, vmem),
        scratch_shapes=[
            pltpu.VMEM((knots_z, 1, knots_y), F32),
            pltpu.VMEM((1, cells_y), jnp.int32),
            pltpu.VMEM((1, cells_y), F32),
            pltpu.VMEM((1, dof_cell.size), jnp.int32),
            pltpu.VMEM(impedance.shape, F32),
            pltpu.VMEM(history.shape, F32),
            pltpu.SMEM(coupling.shape, F32),
            pltpu.SMEM((1, comps), F32),
            pltpu.VMEM((comps, cells_x + 2, cells_y, depth), F32),
            pltpu.VMEM((comps, cells_x + 2, cells_y, depth), F32),
            pltpu.VMEM(plate.shape, BF16),
            pltpu.VMEM((16, 2, 128), F32),
            pltpu.VMEM((16, 16, 128), F32),
            pltpu.VMEM((8, 4, 1, 128), F32),
            pltpu.VMEM((32, 128), F32),
            pltpu.VMEM((32, 128), F32),
            pltpu.VMEM((32, 128), F32),
            pltpu.VMEM((32, 128), F32),
            pltpu.VMEM((32, 128), F32),
            pltpu.VMEM((256, 4096), BF16),
            pltpu.VMEM((1, 4096), jnp.int32),
            pltpu.VMEM((64, 1, 128), F32),
            pltpu.VMEM((2, comps + 1, 8, 128), F32),
            pltpu.VMEM((2, comps + 1, 8, 128), F32),
            pltpu.VMEM((24, 128), F32),
            pltpu.VMEM((2, 16, 128), F32),
            pltpu.VMEM((2, 16, 128), F32),
            pltpu.VMEM((2, 8, 128), F32),
            pltpu.VMEM((4, 8, 128), F32),
            pltpu.VMEM((8, 8, 128), F32),
            pltpu.VMEM((comps, cells_y, depth), F32),
            pltpu.VMEM((comps, cells_y, depth), F32),
            pltpu.VMEM((cells_y, depth), F32),
            pltpu.VMEM((cells_y, depth), F32),
            pltpu.SemaphoreType.DMA((16,)),
            pltpu.SemaphoreType.DMA((19,)),
            pltpu.SemaphoreType.DMA((19,)),
            pltpu.SemaphoreType.REGULAR,
        ],
        compiler_params=pltpu.CompilerParams(collective_id=0, has_side_effects=True, vmem_limit_bytes=VMEM_BYTES),
        name="adjoint_step",
    )(
        *[
            pltpu.with_memory_space_constraint(operand, pltpu.HBM)
            for operand in (
                adjoint, forward, coarse_model.transpose(2, 0, 1), knot_span.reshape(1, -1), knot_frac.reshape(1, -1),
                dof_cell.reshape(1, -1), impedance, history, plate, coupling, damping.reshape(1, -1),
            )
        ]
    )
    results = (updated, grad, reaction)
    updated, grad, reaction = pl.pallas_call(
        store_results,
        out_shape=tuple(jax.ShapeDtypeStruct(a.shape, a.dtype) for a in results),
        in_specs=[anywhere] * 3,
        out_specs=(hbm,) * 3,
        scratch_shapes=[pltpu.SemaphoreType.DMA((3,))],
        name="store_results",
    )(*results)
    return updated, grad.transpose(1, 2, 0), reaction.reshape(-1)


def solution(mesh):
    return jax.shard_map(
        on_device,
        mesh=mesh,
        in_specs=(
            P(None, "gx", "yz", None),
            P(None, "gx", "yz", None),
            P("gx", None, None),
            P("yz"),
            P("yz"),
            P(),
            P(None, "yz"),
            P(None, "yz"),
            P("yz", None),
            P(),
            P(),
        ),
        out_specs=(P(None, "gx", "yz", None), P("gx", None, None), P("yz")),
        check_vma=False,
    )
```

time: 61.5 us -> 78.2 us (1.27)
  Pallas kernels: 51.5 us -> 75.4 us
  local copies, waits for them, and re-layouts: 8.81 us -> 1.98 us
    pallas_call x0 -> x1, Pallas kernels: none -> 25.1 us  [on_device(): pl.pallas_call(store_results, out_shape=tuple((jax.ShapeDtypeStruct(a.sha...]
    unnamed x24 -> x6, local copies, waits for them, and re-layouts: 8.8 us -> 1.98 us
    pallas_call x1, Pallas kernels: 51.5 us -> 50.3 us  [on_device(): pl.pallas_call(kernel, out_shape=(jax.ShapeDtypeStruct(adjoint.shape, F32...]
where the time goes in v2:
time: 78.2 us; the launch traced here: 78 us
  Pallas kernels  75.4 us (96%)
  local copies, waits for them, and re-layouts  1.98 us (3%)
    pallas_call x1, Pallas kernels, on_device(): pl.pallas_call(kernel, out_shape=(jax.ShapeDtypeStruct(adjoint.shape, F32...  50.3 us
    pallas_call x1, Pallas kernels, on_device(): pl.pallas_call(store_results, out_shape=tuple((jax.ShapeDtypeStruct(a.sha...  25.1 us
    unnamed x6, local copies, waits for them, and re-layouts  1.98 us

profile of v2, /device:TPU:1, one launch (start us, length us, event | category | flops | bytes accessed | tf_op | source)
XLA Modules:
  0.0 78.0 jit_solution(10975853903997192065)
XLA Ops:
  0.6 50.3 %adjoint_step.1 = (f32[12,8,16,128]{3,2,1,0:T(8,128)S(1)}, f32[7,1,67]{2,1,0:T(1,128)S(1)}, f32[1,64]{1,0:T(1,128)S(1)}) custom-call(f32[12,8,16,128]{3,2,1,0:T(8,128)} %adjoint.1, f32[12,8,16,128]{3,2,1,0:T(8,128)} %forward.1, f32[7,1,67]{2,1,0:T(1,128)} %bitcast.8, s32[1,16]{1,0:T(1,128)} %bitcast.9, f32[1,16]{1,0:T(1,128)} %bitcast.10, ...), custom_call_target="tpu_custom_call" | custom-call | tf_op jit(solution)/shard_map/adjoint_step/pallas_call | solution.py:506
  51.0 0.0 copy-start
  51.0 0.9 %copy-done = f32[12,8,16,128]{3,2,1,0:T(8,128)} copy-done((f32[12,8,16,128]{3,2,1,0:T(8,128)}, f32[12,8,16,128]{3,2,1,0:T(8,128)S(1)}, u32[]{:S(2)}) %copy-start) | copy-done | bytes 786456
  51.9 0.0 copy-start.1
  51.9 0.6 copy-done.1
  52.5 0.0 copy-start.2
  52.5 0.5 copy-done.2
  53.0 25.1 %store_results.1 = (f32[12,8,16,128]{3,2,1,0:T(8,128)}, f32[7,1,67]{2,1,0:T(1,128)}, f32[1,64]{1,0:T(1,128)}) custom-call(f32[12,8,16,128]{3,2,1,0:T(8,128)} %copy-done, f32[7,1,67]{2,1,0:T(1,128)} %copy-done.1, f32[1,64]{1,0:T(1,128)} %copy-done.2), custom_call_target="tpu_custom_call" | custom-call | tf_op jit(solution)/shard_map/store_results/pallas_call | solution.py:567
Async XLA Ops:
  51.0 0.9 %copy-start = (f32[12,8,16,128]{3,2,1,0:T(8,128)}, f32[12,8,16,128]{3,2,1,0:T(8,128)S(1)}, u32[]{:S(2)}) copy-start(f32[12,8,16,128]{3,2,1,0:T(8,128)S(1)} %get-tuple-element.9.refs_0_) | copy-start | bytes 2359300
  51.9 0.6 copy-start.1
  52.5 0.5 copy-start.2

commit v3 on v2

--- a/solution.py
+++ b/solution.py
@@ -61,7 +61,7 @@
     updated, grad, reaction,
     coarse, span, frac, dof, impedance, history, coupling, damping,
     adj, fwd, plt_buf, cols, surf, taps, taps_all, picked, picked_mate, taps_mate, impulse, one_hot, row_of, react,
-    y_out, y_in, corr, x_out, x_in, grad_c, grad_x, grad_z, face_adj, face_fwd, face_weights, weights_out,
+    y_out, y_in, corr, x_out, x_in, grad_c, grad_x, grad_z, ring_in, far_in, grad_far,
     load_sems, send_sems, recv_sems, credit,
 ):
     gx, yz = lax.axis_index("gx"), lax.axis_index("yz")
@@ -77,20 +77,14 @@
     upper, lower = jnp.logical_and(z_hi == 0, y == 3), jnp.logical_and(z_hi == 1, y == 0)
     jump = jnp.logical_or(upper, lower)
     near_prev, near_next = jnp.logical_and(has_prev, jnp.logical_not(lower)), jnp.logical_and(has_next, jnp.logical_not(upper))
-    z_half = lax.rem(z_lo + 4, 8)
-    half_way = device_at(z_hi * 8 + z_half, y, x, c)
-    across = device_at((1 - z_hi) * 8 + z_half, 3 - y, x, c)
+    facing = device_at(wrap(z + 8, 16), y, x, c)
 
     barrier = pltpu.get_barrier_semaphore()
 
     def greet(device):
         pl.semaphore_signal(barrier, inc=1, device_id=device, device_id_type=MESH)
 
-    greeted = 24 + has_left.astype(jnp.int32) + has_right.astype(jnp.int32) + jump.astype(jnp.int32)
-
-    @pl.when(jump)
-    def _():
-        greet(across)
+    greeted = 24 + has_left.astype(jnp.int32) + has_right.astype(jnp.int32)
 
     for d in (4, -4, 3, -3, 2, -2, 1, -1):
         greet(device_at(wrap(z + d, 16), y, x, c))
@@ -150,9 +144,15 @@
     for d in (4, -4, 3, -3, 2, -2, 1, -1):
         remote(cols.at[z], cols.at[z], 0, device_at(wrap(z + d, 16), y, x, c)).start()
 
-    @pl.when(jump)
-    def _():
-        pl.semaphore_signal(credit, inc=1, device_id=across, device_id_type=MESH)
+    quarter = comps // 4
+    for ring in range(4):
+        part = pl.ds(ring * quarter, quarter)
+        if ring != 3:
+            pl.when(upper)(remote(adjoint.at[part, 7], ring_in, 15, (z_hi * 4 + ring, yz)).start)
+        if ring != 0:
+            pl.when(lower)(remote(adjoint.at[part, 0], ring_in, 15, (z_hi * 4 + ring, yz)).start)
+
+    pl.semaphore_signal(credit, inc=1, device_id=device_at(wrap(z - 4, 16), y, x, c), device_id_type=MESH)
 
     for load in loads[3:]:
         load.wait()
@@ -198,7 +198,6 @@
     depth_span = lax.div(depth, HZ)
     weights_z = spread_basis(iota((8, 128), 0), depth_span, (depth.astype(F32) + 0.5) / HZ - depth_span.astype(F32))
 
-    weights_out[...] = weights_y
     for side, row in ((0, 0), (1, 15)):
         for k in range(comps):
             y_out[side, k] = adj[k, 1:9, row, :]
@@ -213,18 +212,6 @@
     @pl.when(has_right)
     def _():
         to_right.start()
-
-    face = jnp.where(upper, 8, 1)
-    face_copies = (
-        remote(adj.at[:, face], face_adj, 15, half_way),
-        remote(fwd.at[:, face], face_fwd, 16, across),
-        remote(weights_out, face_weights, 17, half_way),
-    )
-
-    @pl.when(jump)
-    def _():
-        for copy in face_copies:
-            copy.start()
 
     @pl.when(yz == 0)
     def _():
@@ -264,22 +251,26 @@
     arrived(cols.at[pl.ds(0, 8)], 0)
     for d in (4, 3, 2, 1):
         slot = wrap(z + d, 16)
-        remote(cols.at[slot], cols.at[slot], 18, device_at(wrap(z - 4, 16), y, x, c)).start()
+        remote(cols.at[slot], cols.at[slot], 19, device_at(wrap(z - 4, 16), y, x, c)).start()
     for d in (-3, -2, -1):
         slot = wrap(z + d, 16)
-        remote(cols.at[slot], cols.at[slot], 18, device_at(wrap(z + 4, 16), y, x, c)).start()
-
-    @pl.when(jump)
-    def _():
-        pl.semaphore_wait(credit, 1)
+        remote(cols.at[slot], cols.at[slot], 19, device_at(wrap(z + 4, 16), y, x, c)).start()
+
+    @pl.when(upper)
+    def _():
+        ring_in[...] = adj[3 * quarter : 4 * quarter, 8]
 
     @pl.when(lower)
     def _():
-        to_prev.start()
-
-    @pl.when(upper)
-    def _():
-        to_next.start()
+        ring_in[...] = adj[0:quarter, 1]
+
+    @pl.when(jnp.logical_not(jump))
+    def _():
+        arrived(ring_in, 15)
+
+    pl.semaphore_wait(credit, 1)
+    around = remote(ring_in, far_in, 16, facing)
+    around.start()
 
     z_first, z_last = iota((16, 128), 1) == 0, iota((16, 128), 1) == 127
     y_first, y_last = iota((16, 128), 0) == 0, iota((16, 128), 0) == 15
@@ -318,7 +309,7 @@
     def _():
         send_back(1, 9, 1, 8, back_next)
 
-    arrived(cols.at[pl.ds(0, 7)], 18)
+    arrived(cols.at[pl.ds(0, 7)], 19)
     surf[yx] = cols[:, 0, :]
     taps_own = cols[0:8, 1, :]
     for k in range(8):
@@ -400,20 +391,8 @@
 
     corr[0:16, :] = corr[0:16, :] + x_in[0] + x_in[1]
     rows = jnp.concatenate([weights_y, y_in[0, comps, 0:1, :], y_in[1, comps, 0:1, :], jnp.zeros((6, 128), F32)], axis=0)
-    grad_c[0] = project(corr[...], rows)
-
-    @pl.when(jump)
-    def _():
-        arrived(face_adj, 15)
-        arrived(face_fwd, 16)
-        arrived(face_weights, 17)
-        product = plane
-        for k in range(comps):
-            product = product + face_adj[k] * face_fwd[k]
-        grad_c[0] = grad_c[0] + project(product, face_weights[...])
-
-    cores = remote(grad_c.at[0], grad_c.at[1], 12, mate)
-    cores.start()
+    grad_c[0, 0] = project(corr[...], rows)
+    grad_c[0, 1] = jnp.zeros((8, 128), F32)
 
     to_mate.wait()
     first, second = jnp.where(c == 0, taps_all[...], taps_mate[...]), jnp.where(c == 0, taps_mate[...], taps_all[...])
@@ -437,22 +416,56 @@
                     remote(react.at[yz], react.at[yz], 9, target).start()
     reaction[...] = jnp.where(c == 0, own_row[:, 0:64], own_row[:, 64:128])
 
+    arrived(far_in, 16)
+    from_upper, from_lower = z_hi == 1, z_hi == 0
+    for ring in range(4):
+        part = pl.ds(ring * quarter, quarter)
+        here = y == ring
+        if ring != 0:
+            pl.when(jnp.logical_and(here, from_upper))(remote(far_in, adj.at[part, 0], 17, (z_hi * 4, yz)).start)
+        if ring != 3:
+            pl.when(jnp.logical_and(here, from_lower))(remote(far_in, adj.at[part, 9], 17, (z_hi * 4 + 3, yz)).start)
+
+    @pl.when(lower)
+    def _():
+        adj[0:quarter, 0] = far_in[...]
+        arrived(adj.at[pl.ds(quarter, 3 * quarter), 0], 17)
+        product = plane
+        for k in range(comps):
+            product = product + adj[k, 0] * fwd[k, 1]
+        grad_c[0, 1] = project(product, weights_y)
+
+    @pl.when(upper)
+    def _():
+        adj[3 * quarter : 4 * quarter, 9] = far_in[...]
+        arrived(adj.at[pl.ds(0, 3 * quarter), 9], 17)
+        product = plane
+        for k in range(comps):
+            product = product + adj[k, 9] * fwd[k, 8]
+        grad_c[0, 1] = project(product, weights_y)
+
+    cores = remote(grad_c.at[0], grad_c.at[1], 12, mate)
+    cores.start()
     cores.wait()
     grad_x[x] = grad_c[0] + grad_c[1]
     for dx in (2, 1, 3):
         remote(grad_x.at[x], grad_x.at[x], 13, device_at(z, y, wrap(x + dx, 4), c)).start()
     arrived(grad_x.at[pl.ds(0, 3)], 13)
-    grad_z[z_lo] = (grad_x[0] + grad_x[1]) + (grad_x[2] + grad_x[3])
+    both = (grad_x[0] + grad_x[1]) + (grad_x[2] + grad_x[3])
+    grad_z[z_lo] = both[0]
+    grad_far[...] = both[1]
+    across = [
+        remote(grad_far, grad_z.at[8 + z_lo], 18, device_at((1 - z_hi) * 8 + k, 3 - y, x, c))
+        for k in range(8)
+    ]
+
+    @pl.when(jump)
+    def _():
+        for copy in across:
+            copy.start()
+
     for d in (7, 6, 5, 4, 3, 2, 1):
         remote(grad_z.at[z_lo], grad_z.at[z_lo], 14, (gx, lax.rem(z_lo + d, 8) * 8 + x * 2 + c)).start()
-
-    @pl.when(lower)
-    def _():
-        arrived(adj.at[:, 0], 2)
-
-    @pl.when(upper)
-    def _():
-        arrived(adj.at[:, 9], 1)
 
     @pl.loop(0, 2)
     def _(side):
@@ -469,23 +482,46 @@
     total = grad_z[0]
     for k in range(1, 8):
         total = total + grad_z[k]
-    total = total / (grad_norm * 4096.0**0.5)
-    for k in range(knots_z):
-        grad[k] = total[k : k + 1, 0:knots_y]
+
+    def put(values):
+        values = values / (grad_norm * 4096.0**0.5)
+        for k in range(knots_z):
+            grad[k] = values[k : k + 1, 0:knots_y]
+
+    @pl.when(jnp.logical_not(jump))
+    def _():
+        put(total)
+
+    @pl.when(jump)
+    def _():
+        arrived(grad_z.at[pl.ds(8, 8)], 18)
+        values = total
+        for k in range(8, 16):
+            values = values + grad_z[k]
+        put(values)
 
     sent(cols.at[pl.ds(0, 8)], 0)
-    sent(cols.at[pl.ds(0, 7)], 18)
+    sent(cols.at[pl.ds(0, 7)], 19)
+    sent(far_in, 16)
     sent(surf.at[pl.ds(0, 15)], 5)
     sent(taps.at[:, pl.ds(0, 3)], 6)
     sent(react.at[pl.ds(0, 63)], 9)
     sent(grad_x.at[pl.ds(0, 3)], 13)
     sent(grad_z.at[pl.ds(0, 7)], 14)
     for present, copy in (
-        (has_prev, to_prev), (has_next, to_next), (has_left, to_left), (has_right, to_right),
+        (near_prev, to_prev), (near_next, to_next), (has_left, to_left), (has_right, to_right),
         (near_prev, back_prev), (near_next, back_next),
-        (jump, face_copies[0]), (jump, face_copies[1]), (jump, face_copies[2]),
     ):
         pl.when(present)(copy.wait_send)
+
+    @pl.when(jump)
+    def _():
+        sent(adj.at[pl.ds(0, 3 * quarter), 0], 15)
+        sent(grad_z.at[pl.ds(0, 8)], 18)
+
+    @pl.when(jnp.logical_not(jump))
+    def _():
+        sent(far_in, 17)
 
 
 def store_results(*refs):
@@ -502,7 +538,6 @@
     knots_y, knots_z = coarse_model.shape[1:]
     vmem = pl.BlockSpec(memory_space=pltpu.VMEM)
     hbm = pl.BlockSpec(memory_space=pltpu.HBM)
-    anywhere = pl.BlockSpec(memory_space=pl.ANY)
     updated, grad, reaction = pl.pallas_call(
         kernel,
         out_shape=(
@@ -540,16 +575,15 @@
             pltpu.VMEM((24, 128), F32),
             pltpu.VMEM((2, 16, 128), F32),
             pltpu.VMEM((2, 16, 128), F32),
-            pltpu.VMEM((2, 8, 128), F32),
-            pltpu.VMEM((4, 8, 128), F32),
-            pltpu.VMEM((8, 8, 128), F32),
-            pltpu.VMEM((comps, cells_y, depth), F32),
-            pltpu.VMEM((comps, cells_y, depth), F32),
-            pltpu.VMEM((cells_y, depth), F32),
-            pltpu.VMEM((cells_y, depth), F32),
+            pltpu.VMEM((2, 2, 8, 128), F32),
+            pltpu.VMEM((4, 2, 8, 128), F32),
+            pltpu.VMEM((16, 8, 128), F32),
+            pltpu.VMEM((comps // 4, cells_y, depth), F32),
+            pltpu.VMEM((comps // 4, cells_y, depth), F32),
+            pltpu.VMEM((8, 128), F32),
             pltpu.SemaphoreType.DMA((16,)),
-            pltpu.SemaphoreType.DMA((19,)),
-            pltpu.SemaphoreType.DMA((19,)),
+            pltpu.SemaphoreType.DMA((20,)),
+            pltpu.SemaphoreType.DMA((20,)),
             pltpu.SemaphoreType.REGULAR,
         ],
         compiler_params=pltpu.CompilerParams(collective_id=0, has_side_effects=True, vmem_limit_bytes=VMEM_BYTES),
@@ -567,7 +601,7 @@
     updated, grad, reaction = pl.pallas_call(
         store_results,
         out_shape=tuple(jax.ShapeDtypeStruct(a.shape, a.dtype) for a in results),
-        in_specs=[anywhere] * 3,
+        in_specs=[vmem] * 3,
         out_specs=(hbm,) * 3,
         scratch_shapes=[pltpu.SemaphoreType.DMA((3,))],
         name="store_results",

time: 78.2 us -> 51.9 us (0.66)
  the two profiles are of different devices: /device:TPU:1 before, /device:TPU:24 now
where the time goes in v3:
time: 51.9 us; the launch traced here: 51.8 us
  Pallas kernels  49.2 us (95%)
  local copies, waits for them, and re-layouts  1.98 us (4%)
  between operations  0.65 us (1%)
    pallas_call x1, Pallas kernels, on_device(): pl.pallas_call(kernel, out_shape=(jax.ShapeDtypeStruct(adjoint.shape, F32...  47.1 us
    pallas_call x1, Pallas kernels, on_device(): pl.pallas_call(store_results, out_shape=tuple((jax.ShapeDtypeStruct(a.sha...  2.05 us
    unnamed x6, local copies, waits for them, and re-layouts  1.98 us

profile of v3, /device:TPU:24, one launch (start us, length us, event | category | flops | bytes accessed | tf_op | source)
XLA Modules:
  0.0 51.8 jit_solution(9864583696177534337)
XLA Ops:
  0.6 47.1 %adjoint_step.1 = (f32[12,8,16,128]{3,2,1,0:T(8,128)S(1)}, f32[7,1,67]{2,1,0:T(1,128)S(1)}, f32[1,64]{1,0:T(1,128)S(1)}) custom-call(f32[12,8,16,128]{3,2,1,0:T(8,128)} %adjoint.1, f32[12,8,16,128]{3,2,1,0:T(8,128)} %forward.1, f32[7,1,67]{2,1,0:T(1,128)} %bitcast.8, s32[1,16]{1,0:T(1,128)} %bitcast.9, f32[1,16]{1,0:T(1,128)} %bitcast.10, ...), custom_call_target="tpu_custom_call" | custom-call | tf_op jit(solution)/shard_map/adjoint_step/pallas_call | solution.py:541
  47.8 0.0 copy-start
  47.8 0.9 %copy-done = f32[12,8,16,128]{3,2,1,0:T(8,128)} copy-done((f32[12,8,16,128]{3,2,1,0:T(8,128)}, f32[12,8,16,128]{3,2,1,0:T(8,128)S(1)}, u32[]{:S(2)}) %copy-start) | copy-done | bytes 786456
  48.6 0.0 copy-start.1
  48.6 0.6 %copy-done.1 = f32[7,1,67]{2,1,0:T(1,128)} copy-done((f32[7,1,67]{2,1,0:T(1,128)}, f32[7,1,67]{2,1,0:T(1,128)S(1)}, u32[]{:S(2)}) %copy-start.1) | copy-done | bytes 1900
  49.2 0.0 copy-start.2
  49.2 0.5 copy-done.2
  49.7 2.0 %store_results.1 = (f32[12,8,16,128]{3,2,1,0:T(8,128)}, f32[7,1,67]{2,1,0:T(1,128)}, f32[1,64]{1,0:T(1,128)}) custom-call(f32[12,8,16,128]{3,2,1,0:T(8,128)} %copy-done, f32[7,1,67]{2,1,0:T(1,128)} %copy-done.1, f32[1,64]{1,0:T(1,128)} %copy-done.2), custom_call_target="tpu_custom_call" | custom-call | tf_op jit(solution)/shard_map/store_results/pallas_call | solution.py:601
Async XLA Ops:
  47.8 0.9 %copy-start = (f32[12,8,16,128]{3,2,1,0:T(8,128)}, f32[12,8,16,128]{3,2,1,0:T(8,128)S(1)}, u32[]{:S(2)}) copy-start(f32[12,8,16,128]{3,2,1,0:T(8,128)S(1)} %get-tuple-element.9.refs_0_) | copy-start | bytes 2359300
  48.6 0.6 %copy-start.1 = (f32[7,1,67]{2,1,0:T(1,128)}, f32[7,1,67]{2,1,0:T(1,128)S(1)}, u32[]{:S(2)}) copy-start(f32[7,1,67]{2,1,0:T(1,128)S(1)} %get-tuple-element.10.refs_1_) | copy-start | bytes 5632
  49.2 0.5 copy-start.2

commit v4 on v3

--- a/solution.py
+++ b/solution.py
@@ -14,6 +14,7 @@
 
 HZ = 32
 VMEM_BYTES = 16 * 1024 * 1024
+STORE_VMEM_BYTES = 4 * 1024 * 1024
 time_step = 0.1
 surface_gain = 40.0
 grad_norm = 20.0
@@ -61,7 +62,7 @@
     updated, grad, reaction,
     coarse, span, frac, dof, impedance, history, coupling, damping,
     adj, fwd, plt_buf, cols, surf, taps, taps_all, picked, picked_mate, taps_mate, impulse, one_hot, row_of, react,
-    y_out, y_in, corr, x_out, x_in, grad_c, grad_x, grad_z, ring_in, far_in, grad_far,
+    y_out, y_in, corr, x_out, x_in, grad_c, grad_x, grad_z, ring_adj, ring_fwd, far_in, grad_far, grad_far_in,
     load_sems, send_sems, recv_sems, credit,
 ):
     gx, yz = lax.axis_index("gx"), lax.axis_index("yz")
@@ -78,29 +79,6 @@
     jump = jnp.logical_or(upper, lower)
     near_prev, near_next = jnp.logical_and(has_prev, jnp.logical_not(lower)), jnp.logical_and(has_next, jnp.logical_not(upper))
     facing = device_at(wrap(z + 8, 16), y, x, c)
-
-    barrier = pltpu.get_barrier_semaphore()
-
-    def greet(device):
-        pl.semaphore_signal(barrier, inc=1, device_id=device, device_id_type=MESH)
-
-    greeted = 24 + has_left.astype(jnp.int32) + has_right.astype(jnp.int32)
-
-    for d in (4, -4, 3, -3, 2, -2, 1, -1):
-        greet(device_at(wrap(z + d, 16), y, x, c))
-    for dy in RING_OFFSETS:
-        for dx in RING_OFFSETS:
-            if (dy, dx) != (0, 0):
-                greet(device_at(z, wrap(y + dy, 4), wrap(x + dx, 4), c))
-    greet(mate)
-
-    @pl.when(has_left)
-    def _():
-        greet((gx, yz - 1))
-
-    @pl.when(has_right)
-    def _():
-        greet((gx, yz + 1))
 
     loads = [
         pltpu.make_async_copy(adjoint.at[2], adj.at[2, pl.ds(1, 8)], load_sems.at[0]),
@@ -120,6 +98,29 @@
     for load in loads:
         load.start()
 
+    barrier = pltpu.get_barrier_semaphore()
+
+    def greet(device):
+        pl.semaphore_signal(barrier, inc=1, device_id=device, device_id_type=MESH)
+
+    greeted = 24 + has_left.astype(jnp.int32) + has_right.astype(jnp.int32)
+
+    for d in (4, -4, 3, -3, 2, -2, 1, -1):
+        greet(device_at(wrap(z + d, 16), y, x, c))
+    for dy in RING_OFFSETS:
+        for dx in RING_OFFSETS:
+            if (dy, dx) != (0, 0):
+                greet(device_at(z, wrap(y + dy, 4), wrap(x + dx, 4), c))
+    greet(mate)
+
+    @pl.when(has_left)
+    def _():
+        greet((gx, yz - 1))
+
+    @pl.when(has_right)
+    def _():
+        greet((gx, yz + 1))
+
     loads[1].wait()
     loads[2].wait()
     tail = jnp.sum(impedance[1:, :] * history[...], axis=0, keepdims=True)
@@ -145,18 +146,19 @@
         remote(cols.at[z], cols.at[z], 0, device_at(wrap(z + d, 16), y, x, c)).start()
 
     quarter = comps // 4
-    for ring in range(4):
-        part = pl.ds(ring * quarter, quarter)
-        if ring != 3:
-            pl.when(upper)(remote(adjoint.at[part, 7], ring_in, 15, (z_hi * 4 + ring, yz)).start)
-        if ring != 0:
-            pl.when(lower)(remote(adjoint.at[part, 0], ring_in, 15, (z_hi * 4 + ring, yz)).start)
+    for field, buffer, sem in ((adjoint, ring_adj, 15), (forward, ring_fwd, 1)):
+        for ring in range(4):
+            part = pl.ds(ring * quarter, quarter)
+            if ring != 3:
+                pl.when(upper)(remote(field.at[part, 7], buffer, sem, (z_hi * 4 + ring, yz)).start)
+            if ring != 0:
+                pl.when(lower)(remote(field.at[part, 0], buffer, sem, (z_hi * 4 + ring, yz)).start)
 
     pl.semaphore_signal(credit, inc=1, device_id=device_at(wrap(z - 4, 16), y, x, c), device_id_type=MESH)
 
     for load in loads[3:]:
         load.wait()
-    to_prev = remote(adj.at[:, 1], adj.at[:, 9], 1, (lax.max(gx - 1, 0), yz))
+    to_prev = remote(adj.at[:, 1], adj.at[:, 9], 20, (lax.max(gx - 1, 0), yz))
     to_next = remote(adj.at[:, 8], adj.at[:, 0], 2, (lax.min(gx + 1, 7), yz))
 
     @pl.when(near_prev)
@@ -248,6 +250,24 @@
     owner_lane = lax.bitwise_and(owner, 127)
     pick_row = (lax.bitwise_and(iota((128, 128), 1), 63) == owner_row).astype(F32).astype(BF16)
 
+    @pl.when(upper)
+    def _():
+        ring_adj[...] = adj[3 * quarter : 4 * quarter, 8]
+        ring_fwd[...] = fwd[3 * quarter : 4 * quarter, 8]
+
+    @pl.when(lower)
+    def _():
+        ring_adj[...] = adj[0:quarter, 1]
+        ring_fwd[...] = fwd[0:quarter, 1]
+
+    @pl.when(jnp.logical_not(jump))
+    def _():
+        arrived(ring_adj, 15)
+
+    pl.semaphore_wait(credit, 1)
+    around = remote(ring_adj, far_in, 16, facing)
+    around.start()
+
     arrived(cols.at[pl.ds(0, 8)], 0)
     for d in (4, 3, 2, 1):
         slot = wrap(z + d, 16)
@@ -256,22 +276,6 @@
         slot = wrap(z + d, 16)
         remote(cols.at[slot], cols.at[slot], 19, device_at(wrap(z + 4, 16), y, x, c)).start()
 
-    @pl.when(upper)
-    def _():
-        ring_in[...] = adj[3 * quarter : 4 * quarter, 8]
-
-    @pl.when(lower)
-    def _():
-        ring_in[...] = adj[0:quarter, 1]
-
-    @pl.when(jnp.logical_not(jump))
-    def _():
-        arrived(ring_in, 15)
-
-    pl.semaphore_wait(credit, 1)
-    around = remote(ring_in, far_in, 16, facing)
-    around.start()
-
     z_first, z_last = iota((16, 128), 1) == 0, iota((16, 128), 1) == 127
     y_first, y_last = iota((16, 128), 0) == 0, iota((16, 128), 0) == 15
 
@@ -307,7 +311,7 @@
 
     @pl.when(near_next)
     def _():
-        send_back(1, 9, 1, 8, back_next)
+        send_back(1, 9, 20, 8, back_next)
 
     arrived(cols.at[pl.ds(0, 7)], 19)
     surf[yx] = cols[:, 0, :]
@@ -392,7 +396,35 @@
     corr[0:16, :] = corr[0:16, :] + x_in[0] + x_in[1]
     rows = jnp.concatenate([weights_y, y_in[0, comps, 0:1, :], y_in[1, comps, 0:1, :], jnp.zeros((6, 128), F32)], axis=0)
     grad_c[0, 0] = project(corr[...], rows)
-    grad_c[0, 1] = jnp.zeros((8, 128), F32)
+
+    arrived(far_in, 16)
+    for ring in range(4):
+        part = pl.ds(ring * quarter, quarter)
+        here = y == ring
+        if ring != 0:
+            pl.when(jnp.logical_and(here, z_hi == 1))(remote(far_in, adj.at[part, 0], 17, (z_hi * 4, yz)).start)
+        if ring != 3:
+            pl.when(jnp.logical_and(here, z_hi == 0))(remote(far_in, adj.at[part, 9], 17, (z_hi * 4 + 3, yz)).start)
+
+    @pl.when(lower)
+    def _():
+        adj[0:quarter, 0] = far_in[...]
+
+    @pl.when(upper)
+    def _():
+        adj[3 * quarter : 4 * quarter, 9] = far_in[...]
+
+    @pl.when(jnp.logical_not(jump))
+    def _():
+        arrived(ring_fwd, 1)
+
+    product = plane
+    for k in range(quarter):
+        product = product + far_in[k] * ring_fwd[k]
+    grad_c[0, 1] = project(product, weights_y)
+
+    cores = remote(grad_c.at[0], grad_c.at[1], 12, mate)
+    cores.start()
 
     to_mate.wait()
     first, second = jnp.where(c == 0, taps_all[...], taps_mate[...]), jnp.where(c == 0, taps_mate[...], taps_all[...])
@@ -401,6 +433,11 @@
     tails = jnp.where(low_half, pltpu.roll(first, 64, 1), second)
     picks.wait()
     impulse[...] = weight * (picked[...] + picked_mate[...]) + tails
+
+    cores.wait()
+    grad_x[x] = grad_c[0] + grad_c[1]
+    for dx in (2, 1, 3):
+        remote(grad_x.at[x], grad_x.at[x], 13, device_at(z, y, wrap(x + dx, 4), c)).start()
 
     flat = jnp.concatenate([impulse[k : k + 1, :] for k in range(32)], axis=1).astype(BF16)
     through = lax.dot_general(flat, plt_buf[...], (((1,), (1,)), ((), ())), preferred_element_type=F32)
@@ -416,56 +453,23 @@
                     remote(react.at[yz], react.at[yz], 9, target).start()
     reaction[...] = jnp.where(c == 0, own_row[:, 0:64], own_row[:, 64:128])
 
-    arrived(far_in, 16)
-    from_upper, from_lower = z_hi == 1, z_hi == 0
-    for ring in range(4):
-        part = pl.ds(ring * quarter, quarter)
-        here = y == ring
-        if ring != 0:
-            pl.when(jnp.logical_and(here, from_upper))(remote(far_in, adj.at[part, 0], 17, (z_hi * 4, yz)).start)
-        if ring != 3:
-            pl.when(jnp.logical_and(here, from_lower))(remote(far_in, adj.at[part, 9], 17, (z_hi * 4 + 3, yz)).start)
-
-    @pl.when(lower)
-    def _():
-        adj[0:quarter, 0] = far_in[...]
-        arrived(adj.at[pl.ds(quarter, 3 * quarter), 0], 17)
-        product = plane
-        for k in range(comps):
-            product = product + adj[k, 0] * fwd[k, 1]
-        grad_c[0, 1] = project(product, weights_y)
-
-    @pl.when(upper)
-    def _():
-        adj[3 * quarter : 4 * quarter, 9] = far_in[...]
-        arrived(adj.at[pl.ds(0, 3 * quarter), 9], 17)
-        product = plane
-        for k in range(comps):
-            product = product + adj[k, 9] * fwd[k, 8]
-        grad_c[0, 1] = project(product, weights_y)
-
-    cores = remote(grad_c.at[0], grad_c.at[1], 12, mate)
-    cores.start()
-    cores.wait()
-    grad_x[x] = grad_c[0] + grad_c[1]
-    for dx in (2, 1, 3):
-        remote(grad_x.at[x], grad_x.at[x], 13, device_at(z, y, wrap(x + dx, 4), c)).start()
     arrived(grad_x.at[pl.ds(0, 3)], 13)
     both = (grad_x[0] + grad_x[1]) + (grad_x[2] + grad_x[3])
     grad_z[z_lo] = both[0]
     grad_far[...] = both[1]
-    across = [
-        remote(grad_far, grad_z.at[8 + z_lo], 18, device_at((1 - z_hi) * 8 + k, 3 - y, x, c))
-        for k in range(8)
-    ]
-
-    @pl.when(jump)
-    def _():
-        for copy in across:
-            copy.start()
-
+    for k in range(8):
+        target = device_at((1 - z_hi) * 8 + k, jnp.where(z_hi == 1, 3, 0), x, c)
+        remote(grad_far, grad_far_in.at[z_lo * 4 + y], 18, target).start()
     for d in (7, 6, 5, 4, 3, 2, 1):
         remote(grad_z.at[z_lo], grad_z.at[z_lo], 14, (gx, lax.rem(z_lo + d, 8) * 8 + x * 2 + c)).start()
+
+    @pl.when(lower)
+    def _():
+        arrived(adj.at[pl.ds(quarter, 3 * quarter), 0], 17)
+
+    @pl.when(upper)
+    def _():
+        arrived(adj.at[pl.ds(0, 3 * quarter), 9], 17)
 
     @pl.loop(0, 2)
     def _(side):
@@ -494,11 +498,8 @@
 
     @pl.when(jump)
     def _():
-        arrived(grad_z.at[pl.ds(8, 8)], 18)
-        values = total
-        for k in range(8, 16):
-            values = values + grad_z[k]
-        put(values)
+        arrived(grad_far_in, 18)
+        put(total + jnp.sum(grad_far_in[...], axis=0))
 
     sent(cols.at[pl.ds(0, 8)], 0)
     sent(cols.at[pl.ds(0, 7)], 19)
@@ -514,10 +515,12 @@
     ):
         pl.when(present)(copy.wait_send)
 
+    sent(grad_far_in.at[pl.ds(0, 8)], 18)
+
     @pl.when(jump)
     def _():
         sent(adj.at[pl.ds(0, 3 * quarter), 0], 15)
-        sent(grad_z.at[pl.ds(0, 8)], 18)
+        sent(adj.at[pl.ds(0, 3 * quarter), 0], 1)
 
     @pl.when(jnp.logical_not(jump))
     def _():
@@ -577,13 +580,15 @@
             pltpu.VMEM((2, 16, 128), F32),
             pltpu.VMEM((2, 2, 8, 128), F32),
             pltpu.VMEM((4, 2, 8, 128), F32),
-            pltpu.VMEM((16, 8, 128), F32),
+            pltpu.VMEM((8, 8, 128), F32),
+            pltpu.VMEM((comps // 4, cells_y, depth), F32),
             pltpu.VMEM((comps // 4, cells_y, depth), F32),
             pltpu.VMEM((comps // 4, cells_y, depth), F32),
             pltpu.VMEM((8, 128), F32),
+            pltpu.VMEM((32, 8, 128), F32),
             pltpu.SemaphoreType.DMA((16,)),
-            pltpu.SemaphoreType.DMA((20,)),
-            pltpu.SemaphoreType.DMA((20,)),
+            pltpu.SemaphoreType.DMA((21,)),
+            pltpu.SemaphoreType.DMA((21,)),
             pltpu.SemaphoreType.REGULAR,
         ],
         compiler_params=pltpu.CompilerParams(collective_id=0, has_side_effects=True, vmem_limit_bytes=VMEM_BYTES),
@@ -604,6 +609,7 @@
         in_specs=[vmem] * 3,
         out_specs=(hbm,) * 3,
         scratch_shapes=[pltpu.SemaphoreType.DMA((3,))],
+        compiler_params=pltpu.CompilerParams(vmem_limit_bytes=STORE_VMEM_BYTES),
         name="store_results",
     )(*results)
     return updated, grad.transpose(1, 2, 0), reaction.reshape(-1)

time: 51.9 us -> 43.7 us (0.84)
  the two profiles are of different devices: /device:TPU:24 before, /device:TPU:1 now
where the time goes in v4:
time: 43.7 us; the launch traced here: 43.3 us
  Pallas kernels  42.7 us (98%)
  between operations  0.64 us (1%)
    pallas_call x1, Pallas kernels, on_device(): pl.pallas_call(kernel, out_shape=(jax.ShapeDtypeStruct(adjoint.shape, F32...  41.8 us
    pallas_call x1, Pallas kernels, on_device(): pl.pallas_call(store_results, out_shape=tuple((jax.ShapeDtypeStruct(a.sha...  0.91 us

profile of v4, /device:TPU:1, one launch (start us, length us, event | category | flops | bytes accessed | tf_op | source)
XLA Modules:
  0.0 43.3 jit_solution(14469384592639075369)
XLA Ops:
  0.6 41.8 %adjoint_step.1 = (f32[12,8,16,128]{3,2,1,0:T(8,128)S(1)}, f32[7,1,67]{2,1,0:T(1,128)S(1)}, f32[1,64]{1,0:T(1,128)S(1)}) custom-call(f32[12,8,16,128]{3,2,1,0:T(8,128)} %adjoint.1, f32[12,8,16,128]{3,2,1,0:T(8,128)} %forward.1, f32[7,1,67]{2,1,0:T(1,128)} %bitcast.8, s32[1,16]{1,0:T(1,128)} %bitcast.9, f32[1,16]{1,0:T(1,128)} %bitcast.10, ...), custom_call_target="tpu_custom_call" | custom-call | tf_op jit(solution)/shard_map/adjoint_step/pallas_call | solution.py:544
  42.4 0.9 %store_results.1 = (f32[12,8,16,128]{3,2,1,0:T(8,128)}, f32[7,1,67]{2,1,0:T(1,128)}, f32[1,64]{1,0:T(1,128)}) custom-call(f32[12,8,16,128]{3,2,1,0:T(8,128)S(1)} %get-tuple-element.9.refs_0_, f32[7,1,67]{2,1,0:T(1,128)S(1)} %get-tuple-element.10.refs_1_, f32[1,64]{1,0:T(1,128)S(1)} %get-tuple-element.11.refs_2_), custom_call_target="tpu_custom_call" | custom-call | tf_op jit(solution)/shard_map/store_results/pallas_call | solution.py:606

commit v5 on v4

--- a/solution.py
+++ b/solution.py
@@ -21,6 +21,7 @@
 
 NEAR_OFFSETS = tuple(sorted(range(-4, 4), key=lambda d: -abs(d)))
 RING_OFFSETS = (2, 1, 3, 0)
+Z_NEAR = (4, -4, 3, -3, 2, -2, 1, -1)
 
 
 def bspline_weights(param):
@@ -61,8 +62,8 @@
     adjoint, forward, coarse_hbm, span_hbm, frac_hbm, dof_hbm, impedance_hbm, history_hbm, plate, coupling_hbm, damping_hbm,
     updated, grad, reaction,
     coarse, span, frac, dof, impedance, history, coupling, damping,
-    adj, fwd, plt_buf, cols, surf, taps, taps_all, picked, picked_mate, taps_mate, impulse, one_hot, row_of, react,
-    y_out, y_in, corr, x_out, x_in, grad_c, grad_x, grad_z, ring_adj, ring_fwd, far_in, grad_far, grad_far_in,
+    adj, fwd, plt_buf, cols, surf, taps, taps_all, picked, impulse, one_hot, row_of, react,
+    y_out, y_in, corr, x_out, x_in, grad_c, grad_x, grad_z, ring_adj, ring_fwd, mid_adj, mid_fwd, mid_weights, weights_out, far_in, grad_far, grad_far_in,
     load_sems, send_sems, recv_sems, credit,
 ):
     gx, yz = lax.axis_index("gx"), lax.axis_index("yz")
@@ -78,7 +79,8 @@
     upper, lower = jnp.logical_and(z_hi == 0, y == 3), jnp.logical_and(z_hi == 1, y == 0)
     jump = jnp.logical_or(upper, lower)
     near_prev, near_next = jnp.logical_and(has_prev, jnp.logical_not(lower)), jnp.logical_and(has_next, jnp.logical_not(upper))
-    facing = device_at(wrap(z + 8, 16), y, x, c)
+    z_half = lax.rem(z_lo + 4, 8)
+    half_way, across = device_at(z_hi * 8 + z_half, y, x, c), device_at((1 - z_hi) * 8 + z_half, y, x, c)
 
     loads = [
         pltpu.make_async_copy(adjoint.at[2], adj.at[2, pl.ds(1, 8)], load_sems.at[0]),
@@ -87,7 +89,6 @@
         pltpu.make_async_copy(adjoint.at[pl.ds(0, 2)], adj.at[pl.ds(0, 2), pl.ds(1, 8)], load_sems.at[1]),
         pltpu.make_async_copy(adjoint.at[pl.ds(3, 9)], adj.at[pl.ds(3, 9), pl.ds(1, 8)], load_sems.at[2]),
         pltpu.make_async_copy(forward, fwd.at[:, pl.ds(1, 8)], load_sems.at[3]),
-        pltpu.make_async_copy(plate, plt_buf, load_sems.at[4]),
         pltpu.make_async_copy(coarse_hbm, coarse, load_sems.at[10]),
         pltpu.make_async_copy(span_hbm, span, load_sems.at[11]),
         pltpu.make_async_copy(frac_hbm, frac, load_sems.at[12]),
@@ -97,20 +98,36 @@
     ]
     for load in loads:
         load.start()
+    leads, follows = c == 1, c == 0
+    share = plate.shape[0]
+    own_plate = pltpu.make_async_copy(plate, plt_buf.at[pl.ds(share, share)], load_sems.at[4])
+    pl.when(leads)(own_plate.start)
 
     barrier = pltpu.get_barrier_semaphore()
 
     def greet(device):
         pl.semaphore_signal(barrier, inc=1, device_id=device, device_id_type=MESH)
 
-    greeted = 24 + has_left.astype(jnp.int32) + has_right.astype(jnp.int32)
-
-    for d in (4, -4, 3, -3, 2, -2, 1, -1):
-        greet(device_at(wrap(z + d, 16), y, x, c))
-    for dy in RING_OFFSETS:
-        for dx in RING_OFFSETS:
-            if (dy, dx) != (0, 0):
-                greet(device_at(z, wrap(y + dy, 4), wrap(x + dx, 4), c))
+    greeted = jnp.where(leads, 24, 17) + has_left.astype(jnp.int32) + has_right.astype(jnp.int32)
+
+    @pl.when(leads)
+    def _():
+        for d in Z_NEAR:
+            greet(device_at(wrap(z + d, 16), y, x, 1))
+            greet(device_at(wrap(z + d, 16), y, x, 0))
+        for dy in RING_OFFSETS:
+            for dx in RING_OFFSETS:
+                if (dy, dx) != (0, 0):
+                    greet(device_at(z, wrap(y + dy, 4), wrap(x + dx, 4), 1))
+
+    @pl.when(follows)
+    def _():
+        for d in (4, -4):
+            greet(device_at(wrap(z + d, 16), y, x, 0))
+        for d in (2, 1, 3):
+            greet(device_at(z, wrap(y + d, 4), x, 0))
+            greet(device_at(z, y, wrap(x + d, 4), 0))
+
     greet(mate)
 
     @pl.when(has_left)
@@ -124,10 +141,10 @@
     loads[1].wait()
     loads[2].wait()
     tail = jnp.sum(impedance[1:, :] * history[...], axis=0, keepdims=True)
-    cols[z, 1:2, :] = jnp.concatenate([impedance[0:1, :], tail], axis=1)
+    cols[c, z, 1:2, :] = jnp.concatenate([impedance[0:1, :], tail], axis=1)
     loads[0].wait()
     surface = adj[2, 1:9].reshape(128, 128)
-    cols[z, 0:1, :] = jnp.transpose(surface)[0:1, :]
+    cols[c, z, 0:1, :] = jnp.transpose(surface)[0:1, :]
 
     pl.semaphore_wait(barrier, greeted)
 
@@ -142,8 +159,15 @@
     def sent(ref, sem):
         pltpu.make_async_copy(ref, ref, send_sems.at[sem]).wait()
 
-    for d in (4, -4, 3, -3, 2, -2, 1, -1):
-        remote(cols.at[z], cols.at[z], 0, device_at(wrap(z + d, 16), y, x, c)).start()
+    for core, sem in ((1, 0), (0, 24)):
+        for d in Z_NEAR:
+            pl.when(c == core)(remote(cols.at[core, z], cols.at[core, z], sem, device_at(wrap(z + d, 16), y, x, 1)).start)
+    plate_up = remote(plate, plt_buf.at[pl.ds(0, share)], 7, mate)
+
+    @pl.when(follows)
+    def _():
+        remote(cols.at[0, z], cols.at[0, z], 24, mate).start()
+        plate_up.start()
 
     quarter = comps // 4
     for field, buffer, sem in ((adjoint, ring_adj, 15), (forward, ring_fwd, 1)):
@@ -154,8 +178,6 @@
             if ring != 0:
                 pl.when(lower)(remote(field.at[part, 0], buffer, sem, (z_hi * 4 + ring, yz)).start)
 
-    pl.semaphore_signal(credit, inc=1, device_id=device_at(wrap(z - 4, 16), y, x, c), device_id_type=MESH)
-
     for load in loads[3:]:
         load.wait()
     to_prev = remote(adj.at[:, 1], adj.at[:, 9], 20, (lax.max(gx - 1, 0), yz))
@@ -168,6 +190,14 @@
     @pl.when(near_next)
     def _():
         to_next.start()
+
+    @pl.when(leads)
+    def _():
+        arrived(cols.at[1, pl.ds(0, 8)], 0)
+        arrived(cols.at[0, pl.ds(0, 9)], 24)
+        for d, way in ((4, -4), (3, -4), (2, -4), (1, -4), (-3, 4), (-2, 4), (-1, 4)):
+            slot = wrap(z + d, 16)
+            remote(cols.at[:, slot], cols.at[:, slot], 19, device_at(wrap(z + way, 16), y, x, 1)).start()
 
     plane = jnp.zeros((16, 128), F32)
     for k in range(comps):
@@ -223,21 +253,44 @@
     def _():
         y_in[1] = jnp.zeros_like(y_in[1])
 
+    @pl.when(upper)
+    def _():
+        ring_adj[...] = adj[3 * quarter : 4 * quarter, 8]
+        ring_fwd[...] = fwd[3 * quarter : 4 * quarter, 8]
+
+    @pl.when(lower)
+    def _():
+        ring_adj[...] = adj[0:quarter, 1]
+        ring_fwd[...] = fwd[0:quarter, 1]
+
+    @pl.when(jnp.logical_not(jump))
+    def _():
+        arrived(ring_adj, 15)
+        arrived(ring_fwd, 1)
+
+    weights_out[...] = weights_y
+    remote(ring_adj, mid_adj, 21, half_way).start()
+    remote(ring_fwd, mid_fwd, 22, across).start()
+    remote(weights_out, mid_weights, 23, half_way).start()
+
     cell = dof[...]
-    cell_x, cell_y = lax.shift_right_logical(cell, 10), lax.bitwise_and(cell, 1023)
-    lane = lax.bitwise_and(cell_x, 7) * 16 + lax.bitwise_and(cell_y, 15)
-    cell_gx, cell_yz = lax.shift_right_logical(cell_x, 3), lax.shift_right_logical(cell_y, 4)
-    cell_row = (
-        lax.bitwise_and(cell_gx, 3) * 64
-        + lax.bitwise_and(lax.shift_right_logical(cell_yz, 1), 3) * 16
-        + lax.shift_right_logical(cell_gx, 2) * 8
-        + lax.shift_right_logical(cell_yz, 3)
-    )
-    row_of[...] = jnp.where(lax.bitwise_and(cell_yz, 1) == c, cell_row, -1)
-    for tile in range(16):
-        pattern = (iota((128, 256), 0) == lane[:, tile * 256 : tile * 256 + 256]).astype(F32).astype(BF16)
-        one_hot[0:128, tile * 256 : tile * 256 + 256] = pattern
-        one_hot[128:256, tile * 256 : tile * 256 + 256] = pattern
+
+    @pl.when(leads)
+    def _():
+        cell_x, cell_y = lax.shift_right_logical(cell, 10), lax.bitwise_and(cell, 1023)
+        lane = lax.bitwise_and(cell_x, 7) * 16 + lax.bitwise_and(cell_y, 15)
+        cell_gx, cell_yz = lax.shift_right_logical(cell_x, 3), lax.shift_right_logical(cell_y, 4)
+        cell_row = (
+            lax.bitwise_and(cell_gx, 3) * 64
+            + lax.bitwise_and(lax.shift_right_logical(cell_yz, 1), 3) * 16
+            + lax.shift_right_logical(cell_gx, 2) * 8
+            + lax.shift_right_logical(cell_yz, 3)
+        )
+        row_of[...] = lax.bitwise_and(cell_yz, 1) * 256 + cell_row
+        for tile in range(16):
+            pattern = (iota((128, 256), 0) == lane[:, tile * 256 : tile * 256 + 256]).astype(F32).astype(BF16)
+            one_hot[0:128, tile * 256 : tile * 256 + 256] = pattern
+            one_hot[128:256, tile * 256 : tile * 256 + 256] = pattern
 
     cell_rank = iota((128, 1), 0)
     cell_id = (gx * 8 + lax.shift_right_logical(cell_rank, 4)) * 1024 + yz * 16 + lax.bitwise_and(cell_rank, 15)
@@ -246,35 +299,13 @@
         label = (iota((1, 128), 1) + (tile * 128 + 1)).astype(F32)
         found = found + jnp.where(cell[:, tile * 128 : tile * 128 + 128] == cell_id, label, 0.0)
     owner = jnp.sum(found, axis=1, keepdims=True).astype(jnp.int32) - 1
-    owner_row = lax.shift_right_arithmetic(owner, 6)
+    owner_row = lax.shift_right_arithmetic(owner, 7)
     owner_lane = lax.bitwise_and(owner, 127)
-    pick_row = (lax.bitwise_and(iota((128, 128), 1), 63) == owner_row).astype(F32).astype(BF16)
-
-    @pl.when(upper)
-    def _():
-        ring_adj[...] = adj[3 * quarter : 4 * quarter, 8]
-        ring_fwd[...] = fwd[3 * quarter : 4 * quarter, 8]
-
-    @pl.when(lower)
-    def _():
-        ring_adj[...] = adj[0:quarter, 1]
-        ring_fwd[...] = fwd[0:quarter, 1]
-
-    @pl.when(jnp.logical_not(jump))
-    def _():
-        arrived(ring_adj, 15)
-
-    pl.semaphore_wait(credit, 1)
-    around = remote(ring_adj, far_in, 16, facing)
-    around.start()
-
-    arrived(cols.at[pl.ds(0, 8)], 0)
-    for d in (4, 3, 2, 1):
-        slot = wrap(z + d, 16)
-        remote(cols.at[slot], cols.at[slot], 19, device_at(wrap(z - 4, 16), y, x, c)).start()
-    for d in (-3, -2, -1):
-        slot = wrap(z + d, 16)
-        remote(cols.at[slot], cols.at[slot], 19, device_at(wrap(z + 4, 16), y, x, c)).start()
+    pick_row = (lax.bitwise_and(iota((128, 64), 1), 31) == owner_row).astype(F32).astype(BF16)
+
+    def project(cells, rows):
+        part = lax.dot_general(weights_z, cells, (((1,), (1,)), ((), ())), precision=HIGH, preferred_element_type=F32)
+        return jnp.dot(part, rows, precision=HIGH, preferred_element_type=F32)
 
     z_first, z_last = iota((16, 128), 1) == 0, iota((16, 128), 1) == 127
     y_first, y_last = iota((16, 128), 0) == 0, iota((16, 128), 0) == 15
@@ -313,17 +344,21 @@
     def _():
         send_back(1, 9, 20, 8, back_next)
 
-    arrived(cols.at[pl.ds(0, 7)], 19)
-    surf[yx] = cols[:, 0, :]
-    taps_own = cols[0:8, 1, :]
-    for k in range(8):
-        taps[k, x] = taps_own[k : k + 1, :]
-    for dy in RING_OFFSETS:
-        for dx in RING_OFFSETS:
-            if (dy, dx) != (0, 0):
-                remote(surf.at[yx], surf.at[yx], 5, device_at(z, wrap(y + dy, 4), wrap(x + dx, 4), c)).start()
-    for dx in (2, 1, 3):
-        remote(taps.at[:, x], taps.at[:, x], 6, device_at(z, y, wrap(x + dx, 4), c)).start()
+    @pl.when(leads)
+    def _():
+        arrived(cols.at[:, pl.ds(0, 7)], 19)
+        for core in (0, 1):
+            surf[core, yx] = cols[core, :, 0, :]
+        for dy in RING_OFFSETS:
+            for dx in RING_OFFSETS:
+                if (dy, dx) != (0, 0):
+                    remote(surf.at[:, yx], surf.at[:, yx], 5, device_at(z, wrap(y + dy, 4), wrap(x + dx, 4), 1)).start()
+        for core in (0, 1):
+            taps_own = cols[core, 0:8, 1, :]
+            for k in range(8):
+                taps[k, x, core : core + 1, :] = taps_own[k : k + 1, :]
+        for dx in (2, 1, 3):
+            remote(taps.at[:, x], taps.at[:, x], 6, device_at(z, y, wrap(x + dx, 4), 1)).start()
 
     @pl.when(has_left)
     def _():
@@ -363,23 +398,15 @@
     def _(i):
         update(i)
 
-    arrived(taps.at[:, pl.ds(0, 3)], 6)
-    for k in range(32):
-        taps_all[k : k + 1, :] = taps[k // 4, k % 4]
-    to_mate = remote(taps_all, taps_mate, 7, mate)
-    to_mate.start()
-
-    arrived(surf.at[pl.ds(0, 15)], 5)
-    head, rest = split(surf[...].reshape(256, 128))
-    samples = jnp.concatenate([head, rest], axis=1)
-    for tile in range(16):
-        lanes = slice(tile * 256, tile * 256 + 256)
-        match = jnp.dot(samples, one_hot[:, lanes], preferred_element_type=F32)
-        mine = jnp.sum(jnp.where(iota((256, 256), 0) == row_of[:, lanes], match, 0.0), axis=0, keepdims=True)
-        picked[2 * tile : 2 * tile + 1, :] = mine[:, 0:128]
-        picked[2 * tile + 1 : 2 * tile + 2, :] = mine[:, 128:256]
-    picks = remote(picked, picked_mate, 8, mate)
-    picks.start()
+    arrived(mid_adj, 21)
+    onward = remote(mid_adj, far_in, 16, across)
+    onward.start()
+    arrived(mid_fwd, 22)
+    arrived(mid_weights, 23)
+    product = plane
+    for k in range(quarter):
+        product = product + mid_adj[k] * mid_fwd[k]
+    grad_c[0, 1] = project(product, mid_weights[...])
 
     @pl.when(near_prev)
     def _():
@@ -388,14 +415,76 @@
     @pl.when(near_next)
     def _():
         arrived(x_in.at[1], 10)
-
-    def project(cells, rows):
-        part = lax.dot_general(weights_z, cells, (((1,), (1,)), ((), ())), precision=HIGH, preferred_element_type=F32)
-        return jnp.dot(part, rows, precision=HIGH, preferred_element_type=F32)
 
     corr[0:16, :] = corr[0:16, :] + x_in[0] + x_in[1]
     rows = jnp.concatenate([weights_y, y_in[0, comps, 0:1, :], y_in[1, comps, 0:1, :], jnp.zeros((6, 128), F32)], axis=0)
     grad_c[0, 0] = project(corr[...], rows)
+
+    from_mate = remote(grad_c.at[0], grad_c.at[1], 12, mate)
+    pl.when(leads)(from_mate.start)
+
+    flat_row = lax.div(yz, 2)
+
+    @pl.when(leads)
+    def _():
+        arrived(taps.at[:, pl.ds(0, 3)], 6)
+        for k in range(32):
+            for core in (0, 1):
+                taps_all[core, k : k + 1, :] = taps[k // 4, k % 4, core : core + 1, :]
+        first, second = taps_all[0], taps_all[1]
+        low_half = iota((32, 128), 1) < 64
+        taps_all[0] = jnp.where(low_half, first, pltpu.roll(second, 64, 1))
+        taps_all[1] = jnp.where(low_half, pltpu.roll(first, 64, 1), second)
+
+        arrived(surf.at[:, pl.ds(0, 15)], 5)
+        pl.semaphore_signal(credit, inc=1, device_id=mate, device_id_type=MESH)
+        head, rest = split(surf[...].reshape(512, 128))
+        samples = jnp.concatenate([head, rest], axis=1)
+        for tile in range(16):
+            lanes = slice(tile * 256, tile * 256 + 256)
+            match = jnp.dot(samples, one_hot[:, lanes], preferred_element_type=F32)
+            mine = jnp.sum(jnp.where(iota((512, 256), 0) == row_of[:, lanes], match, 0.0), axis=0, keepdims=True)
+            picked[2 * tile : 2 * tile + 1, :] = mine[:, 0:128]
+            picked[2 * tile + 1 : 2 * tile + 2, :] = mine[:, 128:256]
+        impulse[...] = taps_all[0] * picked[...] + taps_all[1]
+        flat = jnp.concatenate([impulse[k : k + 1, :] for k in range(32)], axis=1).astype(BF16)
+        own_plate.wait()
+        arrived(plt_buf.at[pl.ds(0, share)], 7)
+        through = lax.dot_general(flat, plt_buf[...], (((1,), (1,)), ((), ())), preferred_element_type=F32)
+        react[flat_row] = through + impulse[pl.ds(flat_row, 1), :]
+        for dz in NEAR_OFFSETS:
+            for dx in RING_OFFSETS:
+                for core in (0, 1):
+                    if (dz, dx, core) != (0, 0, 1):
+                        target = device_at(wrap(z - dz, 16), y, wrap(x + dx, 4), core)
+                        remote(react.at[flat_row], react.at[flat_row], 9, target).start()
+
+    @pl.when(follows)
+    def _():
+        from_mate.wait_recv()
+        grad_x[x] = grad_c[0] + grad_c[1]
+        for dx in (2, 1, 3):
+            remote(grad_x.at[x], grad_x.at[x], 13, device_at(z, y, wrap(x + dx, 4), c)).start()
+
+    @pl.when(follows)
+    def _():
+        arrived(grad_x.at[pl.ds(0, 3)], 13)
+        pl.semaphore_wait(credit, 1)
+        both = (grad_x[0] + grad_x[1]) + (grad_x[2] + grad_x[3])
+        grad_z[z_lo] = jnp.where(jump, both[0] + both[1], both[0])
+        grad_far[...] = both[1]
+
+        @pl.when(jnp.logical_not(jump))
+        def _():
+            for k in range(8):
+                for core in (0, 1):
+                    target = device_at(z_hi * 8 + k, jnp.where(z_hi == 0, 3, 0), x, core)
+                    remote(grad_far, grad_far_in.at[z_lo * 3 + y - z_hi], 18, target).start()
+
+        for d in (7, 6, 5, 4, 3, 2, 1, 0):
+            for core in (0, 1):
+                if (d, core) != (0, 0):
+                    remote(grad_z.at[z_lo], grad_z.at[z_lo], 14, (gx, lax.rem(z_lo + d, 8) * 8 + x * 2 + core)).start()
 
     arrived(far_in, 16)
     for ring in range(4):
@@ -414,55 +503,6 @@
     def _():
         adj[3 * quarter : 4 * quarter, 9] = far_in[...]
 
-    @pl.when(jnp.logical_not(jump))
-    def _():
-        arrived(ring_fwd, 1)
-
-    product = plane
-    for k in range(quarter):
-        product = product + far_in[k] * ring_fwd[k]
-    grad_c[0, 1] = project(product, weights_y)
-
-    cores = remote(grad_c.at[0], grad_c.at[1], 12, mate)
-    cores.start()
-
-    to_mate.wait()
-    first, second = jnp.where(c == 0, taps_all[...], taps_mate[...]), jnp.where(c == 0, taps_mate[...], taps_all[...])
-    low_half = iota((32, 128), 1) < 64
-    weight = jnp.where(low_half, first, pltpu.roll(second, 64, 1))
-    tails = jnp.where(low_half, pltpu.roll(first, 64, 1), second)
-    picks.wait()
-    impulse[...] = weight * (picked[...] + picked_mate[...]) + tails
-
-    cores.wait()
-    grad_x[x] = grad_c[0] + grad_c[1]
-    for dx in (2, 1, 3):
-        remote(grad_x.at[x], grad_x.at[x], 13, device_at(z, y, wrap(x + dx, 4), c)).start()
-
-    flat = jnp.concatenate([impulse[k : k + 1, :] for k in range(32)], axis=1).astype(BF16)
-    through = lax.dot_general(flat, plt_buf[...], (((1,), (1,)), ((), ())), preferred_element_type=F32)
-    through = jnp.concatenate([through, through], axis=1)
-    own_half = lax.div(iota((1, 128), 1), 64) == c
-    own_row = jnp.where(own_half, through + impulse[pl.ds(lax.div(yz, 2), 1), :], 0.0)
-    react[yz] = own_row
-    for dz in NEAR_OFFSETS:
-        for dx in RING_OFFSETS:
-            for dc in (1, 0):
-                if (dz, dx, dc) != (0, 0, 0):
-                    target = device_at(wrap(z - dz, 16), y, wrap(x + dx, 4), wrap(c + dc, 2))
-                    remote(react.at[yz], react.at[yz], 9, target).start()
-    reaction[...] = jnp.where(c == 0, own_row[:, 0:64], own_row[:, 64:128])
-
-    arrived(grad_x.at[pl.ds(0, 3)], 13)
-    both = (grad_x[0] + grad_x[1]) + (grad_x[2] + grad_x[3])
-    grad_z[z_lo] = both[0]
-    grad_far[...] = both[1]
-    for k in range(8):
-        target = device_at((1 - z_hi) * 8 + k, jnp.where(z_hi == 1, 3, 0), x, c)
-        remote(grad_far, grad_far_in.at[z_lo * 4 + y], 18, target).start()
-    for d in (7, 6, 5, 4, 3, 2, 1):
-        remote(grad_z.at[z_lo], grad_z.at[z_lo], 14, (gx, lax.rem(z_lo + d, 8) * 8 + x * 2 + c)).start()
-
     @pl.when(lower)
     def _():
         arrived(adj.at[pl.ds(quarter, 3 * quarter), 0], 17)
@@ -475,14 +515,30 @@
     def _(side):
         update(1 + 7 * side)
 
-    arrived(react.at[pl.ds(0, 63)], 9)
-    head, rest = split(react[...].reshape(64, 128))
+    @pl.when(follows)
+    def _():
+        arrived(react, 9)
+
+    @pl.when(leads)
+    def _():
+        arrived(react.at[pl.ds(0, 31)], 9)
+
+    own_row = react[flat_row]
+    reaction[...] = jnp.where(follows, own_row[:, 0:64], own_row[:, 64:128])
+    head, rest = split(react[...].reshape(32, 128))
     forces = jnp.dot(pick_row, jnp.concatenate([head, rest], axis=0), preferred_element_type=F32)
     forces = jnp.sum(jnp.where(iota((128, 128), 1) == owner_lane, forces, 0.0), axis=1, keepdims=True)
     forces = (time_step * surface_gain) * forces.reshape(8, 16, 1)
     updated[2] = updated[2] + jnp.where(iota((8, 16, 128), 2) == 0, forces, 0.0)
 
-    arrived(grad_z.at[pl.ds(0, 7)], 14)
+    @pl.when(leads)
+    def _():
+        arrived(grad_z, 14)
+
+    @pl.when(follows)
+    def _():
+        arrived(grad_z.at[pl.ds(0, 7)], 14)
+
     total = grad_z[0]
     for k in range(1, 8):
         total = total + grad_z[k]
@@ -501,21 +557,37 @@
         arrived(grad_far_in, 18)
         put(total + jnp.sum(grad_far_in[...], axis=0))
 
-    sent(cols.at[pl.ds(0, 8)], 0)
-    sent(cols.at[pl.ds(0, 7)], 19)
+    @pl.when(leads)
+    def _():
+        sent(cols.at[1, pl.ds(0, 8)], 0)
+        sent(cols.at[:, pl.ds(0, 7)], 19)
+        sent(surf.at[:, pl.ds(0, 15)], 5)
+        sent(taps.at[:, pl.ds(0, 3)], 6)
+        sent(react.at[pl.ds(0, 31)], 9)
+        sent(react, 9)
+        from_mate.wait_send()
+
+    @pl.when(follows)
+    def _():
+        sent(cols.at[0, pl.ds(0, 9)], 24)
+        sent(plt_buf.at[pl.ds(0, share)], 7)
+        sent(grad_x.at[pl.ds(0, 3)], 13)
+        sent(grad_far_in.at[pl.ds(0, 15)], 14)
+
+        @pl.when(jnp.logical_not(jump))
+        def _():
+            sent(grad_far_in.at[pl.ds(0, 16)], 18)
+
     sent(far_in, 16)
-    sent(surf.at[pl.ds(0, 15)], 5)
-    sent(taps.at[:, pl.ds(0, 3)], 6)
-    sent(react.at[pl.ds(0, 63)], 9)
-    sent(grad_x.at[pl.ds(0, 3)], 13)
-    sent(grad_z.at[pl.ds(0, 7)], 14)
+    sent(ring_adj, 21)
+    sent(ring_fwd, 22)
+    sent(weights_out, 23)
     for present, copy in (
         (near_prev, to_prev), (near_next, to_next), (has_left, to_left), (has_right, to_right),
         (near_prev, back_prev), (near_next, back_next),
     ):
         pl.when(present)(copy.wait_send)
 
-    sent(grad_far_in.at[pl.ds(0, 8)], 18)
 
     @pl.when(jump)
     def _():
@@ -561,18 +633,16 @@
             pltpu.SMEM((1, comps), F32),
             pltpu.VMEM((comps, cells_x + 2, cells_y, depth), F32),
             pltpu.VMEM((comps, cells_x + 2, cells_y, depth), F32),
-            pltpu.VMEM(plate.shape, BF16),
-            pltpu.VMEM((16, 2, 128), F32),
-            pltpu.VMEM((16, 16, 128), F32),
-            pltpu.VMEM((8, 4, 1, 128), F32),
-            pltpu.VMEM((32, 128), F32),
-            pltpu.VMEM((32, 128), F32),
-            pltpu.VMEM((32, 128), F32),
+            pltpu.VMEM((2 * plate.shape[0], plate.shape[1]), BF16),
+            pltpu.VMEM((2, 16, 2, 128), F32),
+            pltpu.VMEM((2, 16, 16, 128), F32),
+            pltpu.VMEM((8, 4, 2, 128), F32),
+            pltpu.VMEM((2, 32, 128), F32),
             pltpu.VMEM((32, 128), F32),
             pltpu.VMEM((32, 128), F32),
             pltpu.VMEM((256, 4096), BF16),
             pltpu.VMEM((1, 4096), jnp.int32),
-            pltpu.VMEM((64, 1, 128), F32),
+            pltpu.VMEM((32, 1, 128), F32),
             pltpu.VMEM((2, comps + 1, 8, 128), F32),
             pltpu.VMEM((2, comps + 1, 8, 128), F32),
             pltpu.VMEM((24, 128), F32),
@@ -584,11 +654,15 @@
             pltpu.VMEM((comps // 4, cells_y, depth), F32),
             pltpu.VMEM((comps // 4, cells_y, depth), F32),
             pltpu.VMEM((comps // 4, cells_y, depth), F32),
+            pltpu.VMEM((comps // 4, cells_y, depth), F32),
+            pltpu.VMEM((cells_y, depth), F32),
+            pltpu.VMEM((cells_y, depth), F32),
+            pltpu.VMEM((comps // 4, cells_y, depth), F32),
             pltpu.VMEM((8, 128), F32),
-            pltpu.VMEM((32, 8, 128), F32),
+            pltpu.VMEM((24, 8, 128), F32),
             pltpu.SemaphoreType.DMA((16,)),
-            pltpu.SemaphoreType.DMA((21,)),
-            pltpu.SemaphoreType.DMA((21,)),
+            pltpu.SemaphoreType.DMA((25,)),
+            pltpu.SemaphoreType.DMA((25,)),
             pltpu.SemaphoreType.REGULAR,
         ],
         compiler_params=pltpu.CompilerParams(collective_id=0, has_side_effects=True, vmem_limit_bytes=VMEM_BYTES),

time: 43.7 us -> 40.3 us (0.922)
  Pallas kernels: 42.7 us -> 39.5 us
    pallas_call x1, Pallas kernels: 41.8 us -> 38.6 us  [on_device(): pl.pallas_call(kernel, out_shape=(jax.ShapeDtypeStruct(adjoint.shape, F32...]
where the time goes in v5:
time: 40.3 us; the launch traced here: 40.1 us
  Pallas kernels  39.5 us (98%)
  between operations  0.64 us (2%)
    pallas_call x1, Pallas kernels, on_device(): pl.pallas_call(kernel, out_shape=(jax.ShapeDtypeStruct(adjoint.shape, F32...  38.6 us
    pallas_call x1, Pallas kernels, on_device(): pl.pallas_call(store_results, out_shape=tuple((jax.ShapeDtypeStruct(a.sha...  0.91 us

profile of v5, /device:TPU:1, one launch (start us, length us, event | category | flops | bytes accessed | tf_op | source)
XLA Modules:
  0.0 40.1 jit_solution(17442173261187200925)
XLA Ops:
  0.6 38.6 %adjoint_step.1 = (f32[12,8,16,128]{3,2,1,0:T(8,128)S(1)}, f32[7,1,67]{2,1,0:T(1,128)S(1)}, f32[1,64]{1,0:T(1,128)S(1)}) custom-call(f32[12,8,16,128]{3,2,1,0:T(8,128)} %adjoint.1, f32[12,8,16,128]{3,2,1,0:T(8,128)} %forward.1, f32[7,1,67]{2,1,0:T(1,128)} %bitcast.8, s32[1,16]{1,0:T(1,128)} %bitcast.9, f32[1,16]{1,0:T(1,128)} %bitcast.10, ...), custom_call_target="tpu_custom_call" | custom-call | tf_op jit(solution)/shard_map/adjoint_step/pallas_call | solution.py:616
  39.2 0.9 %store_results.1 = (f32[12,8,16,128]{3,2,1,0:T(8,128)}, f32[7,1,67]{2,1,0:T(1,128)}, f32[1,64]{1,0:T(1,128)}) custom-call(f32[12,8,16,128]{3,2,1,0:T(8,128)S(1)} %get-tuple-element.9.refs_0_, f32[7,1,67]{2,1,0:T(1,128)S(1)} %get-tuple-element.10.refs_1_, f32[1,64]{1,0:T(1,128)S(1)} %get-tuple-element.11.refs_2_), custom_call_target="tpu_custom_call" | custom-call | tf_op jit(solution)/shard_map/store_results/pallas_call | solution.py:680

commit v6 on v5

--- a/solution.py
+++ b/solution.py
@@ -62,9 +62,9 @@
     adjoint, forward, coarse_hbm, span_hbm, frac_hbm, dof_hbm, impedance_hbm, history_hbm, plate, coupling_hbm, damping_hbm,
     updated, grad, reaction,
     coarse, span, frac, dof, impedance, history, coupling, damping,
-    adj, fwd, plt_buf, cols, surf, taps, taps_all, picked, impulse, one_hot, row_of, react,
-    y_out, y_in, corr, x_out, x_in, grad_c, grad_x, grad_z, ring_adj, ring_fwd, mid_adj, mid_fwd, mid_weights, weights_out, far_in, grad_far, grad_far_in,
-    load_sems, send_sems, recv_sems, credit,
+    adj, fwd, plt_buf, cols, taps, taps_all, picked, impulse, one_hot, row_of, react,
+    y_out, y_in, corr, x_out, x_in, grad_c, grad_x, grad_z, ring_adj, ring_fwd, mid_adj, mid_fwd, mid_weights, weights_out, far_in, grad_plane,
+    load_sems, send_sems, recv_sems,
 ):
     gx, yz = lax.axis_index("gx"), lax.axis_index("yz")
     z_hi, y = lax.div(gx, 4), lax.rem(gx, 4)
@@ -80,7 +80,8 @@
     jump = jnp.logical_or(upper, lower)
     near_prev, near_next = jnp.logical_and(has_prev, jnp.logical_not(lower)), jnp.logical_and(has_next, jnp.logical_not(upper))
     z_half = lax.rem(z_lo + 4, 8)
-    half_way, across = device_at(z_hi * 8 + z_half, y, x, c), device_at((1 - z_hi) * 8 + z_half, y, x, c)
+    half_way, across = z_hi * 8 + z_half, (1 - z_hi) * 8 + z_half
+    far_y = jnp.where(z_hi == 0, 3, 0)
 
     loads = [
         pltpu.make_async_copy(adjoint.at[2], adj.at[2, pl.ds(1, 8)], load_sems.at[0]),
@@ -108,26 +109,23 @@
     def greet(device):
         pl.semaphore_signal(barrier, inc=1, device_id=device, device_id_type=MESH)
 
-    greeted = jnp.where(leads, 24, 17) + has_left.astype(jnp.int32) + has_right.astype(jnp.int32)
+    greeted = jnp.where(leads, 24, 26) + has_left.astype(jnp.int32) + has_right.astype(jnp.int32)
 
     @pl.when(leads)
     def _():
         for d in Z_NEAR:
             greet(device_at(wrap(z + d, 16), y, x, 1))
             greet(device_at(wrap(z + d, 16), y, x, 0))
-        for dy in RING_OFFSETS:
-            for dx in RING_OFFSETS:
-                if (dy, dx) != (0, 0):
-                    greet(device_at(z, wrap(y + dy, 4), wrap(x + dx, 4), 1))
 
     @pl.when(follows)
     def _():
         for d in (4, -4):
             greet(device_at(wrap(z + d, 16), y, x, 0))
-        for d in (2, 1, 3):
-            greet(device_at(z, wrap(y + d, 4), x, 0))
-            greet(device_at(z, y, wrap(x + d, 4), 0))
-
+
+    for dy in RING_OFFSETS:
+        for dx in RING_OFFSETS:
+            if (dy, dx) != (0, 0):
+                greet(device_at(z, wrap(y + dy, 4), wrap(x + dx, 4), c))
     greet(mate)
 
     @pl.when(has_left)
@@ -269,9 +267,9 @@
         arrived(ring_fwd, 1)
 
     weights_out[...] = weights_y
-    remote(ring_adj, mid_adj, 21, half_way).start()
-    remote(ring_fwd, mid_fwd, 22, across).start()
-    remote(weights_out, mid_weights, 23, half_way).start()
+    remote(ring_adj, mid_adj.at[c], 21, device_at(half_way, y, x, 0)).start()
+    remote(ring_fwd, mid_fwd.at[c], 22, device_at(across, y, x, 0)).start()
+    remote(weights_out, mid_weights.at[c], 23, device_at(half_way, y, x, 0)).start()
 
     cell = dof[...]
 
@@ -280,17 +278,13 @@
         cell_x, cell_y = lax.shift_right_logical(cell, 10), lax.bitwise_and(cell, 1023)
         lane = lax.bitwise_and(cell_x, 7) * 16 + lax.bitwise_and(cell_y, 15)
         cell_gx, cell_yz = lax.shift_right_logical(cell_x, 3), lax.shift_right_logical(cell_y, 4)
-        cell_row = (
-            lax.bitwise_and(cell_gx, 3) * 64
-            + lax.bitwise_and(lax.shift_right_logical(cell_yz, 1), 3) * 16
-            + lax.shift_right_logical(cell_gx, 2) * 8
-            + lax.shift_right_logical(cell_yz, 3)
-        )
-        row_of[...] = lax.bitwise_and(cell_yz, 1) * 256 + cell_row
+        in_column = jnp.logical_and(lax.bitwise_and(cell_gx, 3) == y, lax.bitwise_and(lax.shift_right_logical(cell_yz, 1), 3) == x)
+        depth_of = lax.shift_right_logical(cell_gx, 2) * 8 + lax.shift_right_logical(cell_yz, 3)
+        row_of[...] = jnp.where(in_column, depth_of, -1)
+        lane = lax.bitwise_and(cell_yz, 1) * 128 + lane
         for tile in range(16):
-            pattern = (iota((128, 256), 0) == lane[:, tile * 256 : tile * 256 + 256]).astype(F32).astype(BF16)
-            one_hot[0:128, tile * 256 : tile * 256 + 256] = pattern
-            one_hot[128:256, tile * 256 : tile * 256 + 256] = pattern
+            lanes = slice(tile * 256, tile * 256 + 256)
+            one_hot[:, lanes] = (iota((256, 256), 0) == lane[:, lanes]).astype(F32).astype(BF16)
 
     cell_rank = iota((128, 1), 0)
     cell_id = (gx * 8 + lax.shift_right_logical(cell_rank, 4)) * 1024 + yz * 16 + lax.bitwise_and(cell_rank, 15)
@@ -347,12 +341,18 @@
     @pl.when(leads)
     def _():
         arrived(cols.at[:, pl.ds(0, 7)], 19)
-        for core in (0, 1):
-            surf[core, yx] = cols[core, :, 0, :]
+        cells = jnp.concatenate(split(jnp.concatenate([cols[0, :, 0, :], cols[1, :, 0, :]], axis=1)), axis=0)
+        for tile in range(16):
+            lanes = slice(tile * 256, tile * 256 + 256)
+            match = jnp.dot(cells, one_hot[:, lanes], preferred_element_type=F32)
+            match = jnp.where(iota((16, 256), 0) == row_of[:, lanes], match[:16] + match[16:], 0.0)
+            mine = jnp.sum(match, axis=0, keepdims=True)
+            picked[yx, 2 * tile : 2 * tile + 1, :] = mine[:, 0:128]
+            picked[yx, 2 * tile + 1 : 2 * tile + 2, :] = mine[:, 128:256]
         for dy in RING_OFFSETS:
             for dx in RING_OFFSETS:
                 if (dy, dx) != (0, 0):
-                    remote(surf.at[:, yx], surf.at[:, yx], 5, device_at(z, wrap(y + dy, 4), wrap(x + dx, 4), 1)).start()
+                    remote(picked.at[yx], picked.at[yx], 5, device_at(z, wrap(y + dy, 4), wrap(x + dx, 4), 1)).start()
         for core in (0, 1):
             taps_own = cols[core, 0:8, 1, :]
             for k in range(8):
@@ -375,6 +375,59 @@
             edge = edge + y_in[side, k] * fwd[k, 1:9, row, :]
         corr[16 + side : 17 + side, :] = jnp.sum(edge, axis=0, keepdims=True)
 
+    @pl.when(near_prev)
+    def _():
+        arrived(x_in.at[0], 11)
+
+    @pl.when(near_next)
+    def _():
+        arrived(x_in.at[1], 10)
+
+    corr[0:16, :] = corr[0:16, :] + x_in[0] + x_in[1]
+    rows = jnp.concatenate([weights_y, y_in[0, comps, 0:1, :], y_in[1, comps, 0:1, :], jnp.zeros((6, 128), F32)], axis=0)
+    grad_c[0] = project(corr[...], rows)
+
+    from_mate = remote(grad_c.at[0], grad_c.at[1], 12, mate)
+    pl.when(leads)(from_mate.start)
+
+    @pl.when(follows)
+    def _():
+        from_mate.wait_recv()
+        grad_x[x] = grad_c[0] + grad_c[1]
+        for dx in (2, 1, 3):
+            remote(grad_x.at[x], grad_x.at[x], 13, device_at(z, y, wrap(x + dx, 4), 0)).start()
+        arrived(mid_adj, 21)
+        for core in (0, 1):
+            remote(mid_adj.at[core], far_in, 16, device_at(across, y, x, core)).start()
+        arrived(mid_fwd, 22)
+        arrived(mid_weights, 23)
+        far_part = jnp.zeros((8, 128), F32)
+        for core in (0, 1):
+            product = plane
+            for k in range(quarter):
+                product = product + mid_adj[core, k] * mid_fwd[core, k]
+            far_part = far_part + project(product, mid_weights[core])
+        grad_plane[yx] = far_part
+        for k in range(4):
+            target = remote(grad_plane.at[yx], grad_plane.at[yx], 18, device_at(z, far_y, k, 0))
+            pl.when(jnp.logical_not(jnp.logical_and(jump, x == k)))(target.start)
+
+    def sum_over_z():
+        arrived(grad_x.at[pl.ds(0, 3)], 13)
+        grad_z[z_lo] = (grad_x[0] + grad_x[1]) + (grad_x[2] + grad_x[3])
+
+        @pl.when(jump)
+        def _():
+            arrived(grad_plane.at[pl.ds(0, 15)], 18)
+            grad_z[z_lo] = grad_z[z_lo] + jnp.sum(grad_plane[...], axis=0)
+
+        for d in (7, 6, 5, 4, 3, 2, 1, 0):
+            for core in (0, 1):
+                if (d, core) != (0, 0):
+                    remote(grad_z.at[z_lo], grad_z.at[z_lo], 14, (gx, lax.rem(z_lo + d, 8) * 8 + x * 2 + core)).start()
+
+    pl.when(jnp.logical_and(follows, jnp.logical_not(jump)))(sum_over_z)
+
     knots_z, _, knots_y = coarse.shape
     material = jnp.zeros((16, 128), F32)
     for k in range(knots_z):
@@ -398,30 +451,7 @@
     def _(i):
         update(i)
 
-    arrived(mid_adj, 21)
-    onward = remote(mid_adj, far_in, 16, across)
-    onward.start()
-    arrived(mid_fwd, 22)
-    arrived(mid_weights, 23)
-    product = plane
-    for k in range(quarter):
-        product = product + mid_adj[k] * mid_fwd[k]
-    grad_c[0, 1] = project(product, mid_weights[...])
-
-    @pl.when(near_prev)
-    def _():
-        arrived(x_in.at[0], 11)
-
-    @pl.when(near_next)
-    def _():
-        arrived(x_in.at[1], 10)
-
-    corr[0:16, :] = corr[0:16, :] + x_in[0] + x_in[1]
-    rows = jnp.concatenate([weights_y, y_in[0, comps, 0:1, :], y_in[1, comps, 0:1, :], jnp.zeros((6, 128), F32)], axis=0)
-    grad_c[0, 0] = project(corr[...], rows)
-
-    from_mate = remote(grad_c.at[0], grad_c.at[1], 12, mate)
-    pl.when(leads)(from_mate.start)
+    pl.when(jnp.logical_and(follows, jump))(sum_over_z)
 
     flat_row = lax.div(yz, 2)
 
@@ -436,17 +466,11 @@
         taps_all[0] = jnp.where(low_half, first, pltpu.roll(second, 64, 1))
         taps_all[1] = jnp.where(low_half, pltpu.roll(first, 64, 1), second)
 
-        arrived(surf.at[:, pl.ds(0, 15)], 5)
-        pl.semaphore_signal(credit, inc=1, device_id=mate, device_id_type=MESH)
-        head, rest = split(surf[...].reshape(512, 128))
-        samples = jnp.concatenate([head, rest], axis=1)
-        for tile in range(16):
-            lanes = slice(tile * 256, tile * 256 + 256)
-            match = jnp.dot(samples, one_hot[:, lanes], preferred_element_type=F32)
-            mine = jnp.sum(jnp.where(iota((512, 256), 0) == row_of[:, lanes], match, 0.0), axis=0, keepdims=True)
-            picked[2 * tile : 2 * tile + 1, :] = mine[:, 0:128]
-            picked[2 * tile + 1 : 2 * tile + 2, :] = mine[:, 128:256]
-        impulse[...] = taps_all[0] * picked[...] + taps_all[1]
+        arrived(picked.at[pl.ds(0, 15)], 5)
+        samples = picked[0]
+        for k in range(1, 16):
+            samples = samples + picked[k]
+        impulse[...] = taps_all[0] * samples + taps_all[1]
         flat = jnp.concatenate([impulse[k : k + 1, :] for k in range(32)], axis=1).astype(BF16)
         own_plate.wait()
         arrived(plt_buf.at[pl.ds(0, share)], 7)
@@ -459,33 +483,6 @@
                         target = device_at(wrap(z - dz, 16), y, wrap(x + dx, 4), core)
                         remote(react.at[flat_row], react.at[flat_row], 9, target).start()
 
-    @pl.when(follows)
-    def _():
-        from_mate.wait_recv()
-        grad_x[x] = grad_c[0] + grad_c[1]
-        for dx in (2, 1, 3):
-            remote(grad_x.at[x], grad_x.at[x], 13, device_at(z, y, wrap(x + dx, 4), c)).start()
-
-    @pl.when(follows)
-    def _():
-        arrived(grad_x.at[pl.ds(0, 3)], 13)
-        pl.semaphore_wait(credit, 1)
-        both = (grad_x[0] + grad_x[1]) + (grad_x[2] + grad_x[3])
-        grad_z[z_lo] = jnp.where(jump, both[0] + both[1], both[0])
-        grad_far[...] = both[1]
-
-        @pl.when(jnp.logical_not(jump))
-        def _():
-            for k in range(8):
-                for core in (0, 1):
-                    target = device_at(z_hi * 8 + k, jnp.where(z_hi == 0, 3, 0), x, core)
-                    remote(grad_far, grad_far_in.at[z_lo * 3 + y - z_hi], 18, target).start()
-
-        for d in (7, 6, 5, 4, 3, 2, 1, 0):
-            for core in (0, 1):
-                if (d, core) != (0, 0):
-                    remote(grad_z.at[z_lo], grad_z.at[z_lo], 14, (gx, lax.rem(z_lo + d, 8) * 8 + x * 2 + core)).start()
-
     arrived(far_in, 16)
     for ring in range(4):
         part = pl.ds(ring * quarter, quarter)
@@ -543,25 +540,15 @@
     for k in range(1, 8):
         total = total + grad_z[k]
 
-    def put(values):
-        values = values / (grad_norm * 4096.0**0.5)
-        for k in range(knots_z):
-            grad[k] = values[k : k + 1, 0:knots_y]
-
-    @pl.when(jnp.logical_not(jump))
-    def _():
-        put(total)
-
-    @pl.when(jump)
-    def _():
-        arrived(grad_far_in, 18)
-        put(total + jnp.sum(grad_far_in[...], axis=0))
+    total = total / (grad_norm * 4096.0**0.5)
+    for k in range(knots_z):
+        grad[k] = total[k : k + 1, 0:knots_y]
 
     @pl.when(leads)
     def _():
         sent(cols.at[1, pl.ds(0, 8)], 0)
         sent(cols.at[:, pl.ds(0, 7)], 19)
-        sent(surf.at[:, pl.ds(0, 15)], 5)
+        sent(picked.at[pl.ds(0, 15)], 5)
         sent(taps.at[:, pl.ds(0, 3)], 6)
         sent(react.at[pl.ds(0, 31)], 9)
         sent(react, 9)
@@ -572,13 +559,11 @@
         sent(cols.at[0, pl.ds(0, 9)], 24)
         sent(plt_buf.at[pl.ds(0, share)], 7)
         sent(grad_x.at[pl.ds(0, 3)], 13)
-        sent(grad_far_in.at[pl.ds(0, 15)], 14)
-
-        @pl.when(jnp.logical_not(jump))
-        def _():
-            sent(grad_far_in.at[pl.ds(0, 16)], 18)
-
-    sent(far_in, 16)
+        sent(grad_plane.at[pl.ds(0, 15)], 14)
+        sent(grad_plane.at[pl.ds(0, 3)], 18)
+        pl.when(jnp.logical_not(jump))(lambda: sent(grad_plane.at[0], 18))
+        sent(mid_adj, 16)
+
     sent(ring_adj, 21)
     sent(ring_fwd, 22)
     sent(weights_out, 23)
@@ -635,10 +620,9 @@
             pltpu.VMEM((comps, cells_x + 2, cells_y, depth), F32),
             pltpu.VMEM((2 * plate.shape[0], plate.shape[1]), BF16),
             pltpu.VMEM((2, 16, 2, 128), F32),
-            pltpu.VMEM((2, 16, 16, 128), F32),
             pltpu.VMEM((8, 4, 2, 128), F32),
             pltpu.VMEM((2, 32, 128), F32),
-            pltpu.VMEM((32, 128), F32),
+            pltpu.VMEM((16, 32, 128), F32),
             pltpu.VMEM((32, 128), F32),
             pltpu.VMEM((256, 4096), BF16),
             pltpu.VMEM((1, 4096), jnp.int32),
@@ -648,22 +632,20 @@
             pltpu.VMEM((24, 128), F32),
             pltpu.VMEM((2, 16, 128), F32),
             pltpu.VMEM((2, 16, 128), F32),
-            pltpu.VMEM((2, 2, 8, 128), F32),
-            pltpu.VMEM((4, 2, 8, 128), F32),
+            pltpu.VMEM((2, 8, 128), F32),
+            pltpu.VMEM((4, 8, 128), F32),
             pltpu.VMEM((8, 8, 128), F32),
             pltpu.VMEM((comps // 4, cells_y, depth), F32),
             pltpu.VMEM((comps // 4, cells_y, depth), F32),
-            pltpu.VMEM((comps // 4, cells_y, depth), F32),
-            pltpu.VMEM((comps // 4, cells_y, depth), F32),
-            pltpu.VMEM((cells_y, depth), F32),
+            pltpu.VMEM((2, comps // 4, cells_y, depth), F32),
+            pltpu.VMEM((2, comps // 4, cells_y, depth), F32),
+            pltpu.VMEM((2, cells_y, depth), F32),
             pltpu.VMEM((cells_y, depth), F32),
             pltpu.VMEM((comps // 4, cells_y, depth), F32),
-            pltpu.VMEM((8, 128), F32),
-            pltpu.VMEM((24, 8, 128), F32),
+            pltpu.VMEM((16, 8, 128), F32),
             pltpu.SemaphoreType.DMA((16,)),
             pltpu.SemaphoreType.DMA((25,)),
             pltpu.SemaphoreType.DMA((25,)),
-            pltpu.SemaphoreType.REGULAR,
         ],
         compiler_params=pltpu.CompilerParams(collective_id=0, has_side_effects=True, vmem_limit_bytes=VMEM_BYTES),
         name="adjoint_step",

time: 40.3 us -> 38.2 us (0.948); the launches traced: 40.1 us -> 37.6 us
  Pallas kernels: 39.5 us -> 37 us
    pallas_call x1, Pallas kernels: 38.6 us -> 36.1 us  [on_device(): pl.pallas_call(kernel, out_shape=(jax.ShapeDtypeStruct(adjoint.shape, F32...]
where the time goes in v6:
time: 38.2 us; the launch traced here: 37.6 us
  Pallas kernels  37 us (97%)
  between operations  0.64 us (2%)
    pallas_call x1, Pallas kernels, on_device(): pl.pallas_call(kernel, out_shape=(jax.ShapeDtypeStruct(adjoint.shape, F32...  36.1 us
    pallas_call x1, Pallas kernels, on_device(): pl.pallas_call(store_results, out_shape=tuple((jax.ShapeDtypeStruct(a.sha...  0.91 us

profile of v6, /device:TPU:1, one launch (start us, length us, event | category | flops | bytes accessed | tf_op | source)
XLA Modules:
  0.0 37.6 jit_solution(6838393052592838899)
XLA Ops:
  0.6 36.1 %adjoint_step.1 = (f32[12,8,16,128]{3,2,1,0:T(8,128)S(1)}, f32[7,1,67]{2,1,0:T(1,128)S(1)}, f32[1,64]{1,0:T(1,128)S(1)}) custom-call(f32[12,8,16,128]{3,2,1,0:T(8,128)} %adjoint.1, f32[12,8,16,128]{3,2,1,0:T(8,128)} %forward.1, f32[7,1,67]{2,1,0:T(1,128)} %bitcast.8, s32[1,16]{1,0:T(1,128)} %bitcast.9, f32[1,16]{1,0:T(1,128)} %bitcast.10, ...), custom_call_target="tpu_custom_call" | custom-call | tf_op jit(solution)/shard_map/adjoint_step/pallas_call | solution.py:601
  36.7 0.9 %store_results.1 = (f32[12,8,16,128]{3,2,1,0:T(8,128)}, f32[7,1,67]{2,1,0:T(1,128)}, f32[1,64]{1,0:T(1,128)}) custom-call(f32[12,8,16,128]{3,2,1,0:T(8,128)S(1)} %get-tuple-element.9.refs_0_, f32[7,1,67]{2,1,0:T(1,128)S(1)} %get-tuple-element.10.refs_1_, f32[1,64]{1,0:T(1,128)S(1)} %get-tuple-element.11.refs_2_), custom_call_target="tpu_custom_call" | custom-call | tf_op jit(solution)/shard_map/store_results/pallas_call | solution.py:662

commit v7 on v6

--- a/solution.py
+++ b/solution.py
@@ -63,7 +63,7 @@
     updated, grad, reaction,
     coarse, span, frac, dof, impedance, history, coupling, damping,
     adj, fwd, plt_buf, cols, taps, taps_all, picked, impulse, one_hot, row_of, react,
-    y_out, y_in, corr, x_out, x_in, grad_c, grad_x, grad_z, ring_adj, ring_fwd, mid_adj, mid_fwd, mid_weights, weights_out, far_in, grad_plane,
+    y_out, y_in, corr, x_out, x_in, grad_c, grad_x, grad_z, ring_adj, ring_fwd, mid_adj, mid_fwd, mid_weights, weights_out, grad_plane,
     load_sems, send_sems, recv_sems,
 ):
     gx, yz = lax.axis_index("gx"), lax.axis_index("yz")
@@ -97,12 +97,11 @@
         pltpu.make_async_copy(coupling_hbm, coupling, load_sems.at[14]),
         pltpu.make_async_copy(damping_hbm, damping, load_sems.at[15]),
     ]
-    for load in loads:
+    for load in loads[:3]:
         load.start()
     leads, follows = c == 1, c == 0
     share = plate.shape[0]
     own_plate = pltpu.make_async_copy(plate, plt_buf.at[pl.ds(share, share)], load_sems.at[4])
-    pl.when(leads)(own_plate.start)
 
     barrier = pltpu.get_barrier_semaphore()
 
@@ -135,6 +134,10 @@
     @pl.when(has_right)
     def _():
         greet((gx, yz + 1))
+
+    for load in loads[3:]:
+        load.start()
+    pl.when(leads)(own_plate.start)
 
     loads[1].wait()
     loads[2].wait()
@@ -165,11 +168,10 @@
     @pl.when(follows)
     def _():
         remote(cols.at[0, z], cols.at[0, z], 24, mate).start()
-        plate_up.start()
 
     quarter = comps // 4
     for field, buffer, sem in ((adjoint, ring_adj, 15), (forward, ring_fwd, 1)):
-        for ring in range(4):
+        for ring in (1, 2, 0, 3):
             part = pl.ds(ring * quarter, quarter)
             if ring != 3:
                 pl.when(upper)(remote(field.at[part, 7], buffer, sem, (z_hi * 4 + ring, yz)).start)
@@ -181,13 +183,11 @@
     to_prev = remote(adj.at[:, 1], adj.at[:, 9], 20, (lax.max(gx - 1, 0), yz))
     to_next = remote(adj.at[:, 8], adj.at[:, 0], 2, (lax.min(gx + 1, 7), yz))
 
-    @pl.when(near_prev)
-    def _():
-        to_prev.start()
-
-    @pl.when(near_next)
-    def _():
-        to_next.start()
+    def send_near():
+        pl.when(near_prev)(to_prev.start)
+        pl.when(near_next)(to_next.start)
+
+    pl.when(follows)(send_near)
 
     @pl.when(leads)
     def _():
@@ -196,6 +196,7 @@
         for d, way in ((4, -4), (3, -4), (2, -4), (1, -4), (-3, 4), (-2, 4), (-1, 4)):
             slot = wrap(z + d, 16)
             remote(cols.at[:, slot], cols.at[:, slot], 19, device_at(wrap(z + way, 16), y, x, 1)).start()
+        send_near()
 
     plane = jnp.zeros((16, 128), F32)
     for k in range(comps):
@@ -271,6 +272,7 @@
     remote(ring_fwd, mid_fwd.at[c], 22, device_at(across, y, x, 0)).start()
     remote(weights_out, mid_weights.at[c], 23, device_at(half_way, y, x, 0)).start()
 
+    pl.when(follows)(plate_up.start)
     cell = dof[...]
 
     @pl.when(leads)
@@ -397,17 +399,15 @@
         for dx in (2, 1, 3):
             remote(grad_x.at[x], grad_x.at[x], 13, device_at(z, y, wrap(x + dx, 4), 0)).start()
         arrived(mid_adj, 21)
+        arrived(mid_fwd, 22)
+        part = pl.ds(y * quarter, quarter)
         for core in (0, 1):
-            remote(mid_adj.at[core], far_in, 16, device_at(across, y, x, core)).start()
-        arrived(mid_fwd, 22)
+            target = device_at(across, 3 - far_y, x, core)
+            pl.when(z_hi == 0)(remote(mid_adj.at[core], adj.at[part, 0], 17, target).start)
+            pl.when(z_hi == 1)(remote(mid_adj.at[core], adj.at[part, 9], 17, target).start)
         arrived(mid_weights, 23)
-        far_part = jnp.zeros((8, 128), F32)
-        for core in (0, 1):
-            product = plane
-            for k in range(quarter):
-                product = product + mid_adj[core, k] * mid_fwd[core, k]
-            far_part = far_part + project(product, mid_weights[core])
-        grad_plane[yx] = far_part
+        products = jnp.sum(mid_adj[...] * mid_fwd[...], axis=1)
+        grad_plane[yx] = project(products.reshape(32, 128), mid_weights[...].reshape(32, 128))
         for k in range(4):
             target = remote(grad_plane.at[yx], grad_plane.at[yx], 18, device_at(z, far_y, k, 0))
             pl.when(jnp.logical_not(jnp.logical_and(jump, x == k)))(target.start)
@@ -483,30 +483,13 @@
                         target = device_at(wrap(z - dz, 16), y, wrap(x + dx, 4), core)
                         remote(react.at[flat_row], react.at[flat_row], 9, target).start()
 
-    arrived(far_in, 16)
-    for ring in range(4):
-        part = pl.ds(ring * quarter, quarter)
-        here = y == ring
-        if ring != 0:
-            pl.when(jnp.logical_and(here, z_hi == 1))(remote(far_in, adj.at[part, 0], 17, (z_hi * 4, yz)).start)
-        if ring != 3:
-            pl.when(jnp.logical_and(here, z_hi == 0))(remote(far_in, adj.at[part, 9], 17, (z_hi * 4 + 3, yz)).start)
-
     @pl.when(lower)
     def _():
-        adj[0:quarter, 0] = far_in[...]
+        arrived(adj.at[:, 0], 17)
 
     @pl.when(upper)
     def _():
-        adj[3 * quarter : 4 * quarter, 9] = far_in[...]
-
-    @pl.when(lower)
-    def _():
-        arrived(adj.at[pl.ds(quarter, 3 * quarter), 0], 17)
-
-    @pl.when(upper)
-    def _():
-        arrived(adj.at[pl.ds(0, 3 * quarter), 9], 17)
+        arrived(adj.at[:, 9], 17)
 
     @pl.loop(0, 2)
     def _(side):
@@ -562,7 +545,7 @@
         sent(grad_plane.at[pl.ds(0, 15)], 14)
         sent(grad_plane.at[pl.ds(0, 3)], 18)
         pl.when(jnp.logical_not(jump))(lambda: sent(grad_plane.at[0], 18))
-        sent(mid_adj, 16)
+        sent(mid_adj, 17)
 
     sent(ring_adj, 21)
     sent(ring_fwd, 22)
@@ -578,10 +561,6 @@
     def _():
         sent(adj.at[pl.ds(0, 3 * quarter), 0], 15)
         sent(adj.at[pl.ds(0, 3 * quarter), 0], 1)
-
-    @pl.when(jnp.logical_not(jump))
-    def _():
-        sent(far_in, 17)
 
 
 def store_results(*refs):
@@ -641,7 +620,6 @@
             pltpu.VMEM((2, comps // 4, cells_y, depth), F32),
             pltpu.VMEM((2, cells_y, depth), F32),
             pltpu.VMEM((cells_y, depth), F32),
-            pltpu.VMEM((comps // 4, cells_y, depth), F32),
             pltpu.VMEM((16, 8, 128), F32),
             pltpu.SemaphoreType.DMA((16,)),
             pltpu.SemaphoreType.DMA((25,)),

time: 38.2 us -> 38.2 us (level); the launches traced: 37.6 us -> 38 us
  Pallas kernels: 37 us -> 37.4 us
    pallas_call x1, Pallas kernels: 36.1 us -> 36.5 us  [on_device(): pl.pallas_call(kernel, out_shape=(jax.ShapeDtypeStruct(adjoint.shape, F32...]
where the time goes in v7:
time: 38.2 us; the launch traced here: 38 us
  Pallas kernels  37.4 us (98%)
  between operations  0.64 us (2%)
    pallas_call x1, Pallas kernels, on_device(): pl.pallas_call(kernel, out_shape=(jax.ShapeDtypeStruct(adjoint.shape, F32...  36.5 us
    pallas_call x1, Pallas kernels, on_device(): pl.pallas_call(store_results, out_shape=tuple((jax.ShapeDtypeStruct(a.sha...  0.91 us

profile of v7, /device:TPU:1, one launch (start us, length us, event | category | flops | bytes accessed | tf_op | source)
XLA Modules:
  0.0 38.0 jit_solution(15227094938960727951)
XLA Ops:
  0.6 36.5 %adjoint_step.1 = (f32[12,8,16,128]{3,2,1,0:T(8,128)S(1)}, f32[7,1,67]{2,1,0:T(1,128)S(1)}, f32[1,64]{1,0:T(1,128)S(1)}) custom-call(f32[12,8,16,128]{3,2,1,0:T(8,128)} %adjoint.1, f32[12,8,16,128]{3,2,1,0:T(8,128)} %forward.1, f32[7,1,67]{2,1,0:T(1,128)} %bitcast.8, s32[1,16]{1,0:T(1,128)} %bitcast.9, f32[1,16]{1,0:T(1,128)} %bitcast.10, ...), custom_call_target="tpu_custom_call" | custom-call | tf_op jit(solution)/shard_map/adjoint_step/pallas_call | solution.py:580
  37.1 0.9 %store_results.1 = (f32[12,8,16,128]{3,2,1,0:T(8,128)}, f32[7,1,67]{2,1,0:T(1,128)}, f32[1,64]{1,0:T(1,128)}) custom-call(f32[12,8,16,128]{3,2,1,0:T(8,128)S(1)} %get-tuple-element.9.refs_0_, f32[7,1,67]{2,1,0:T(1,128)S(1)} %get-tuple-element.10.refs_1_, f32[1,64]{1,0:T(1,128)S(1)} %get-tuple-element.11.refs_2_), custom_call_target="tpu_custom_call" | custom-call | tf_op jit(solution)/shard_map/store_results/pallas_call | solution.py:640

commit v8 on v7

--- a/solution.py
+++ b/solution.py
@@ -288,17 +288,6 @@
             lanes = slice(tile * 256, tile * 256 + 256)
             one_hot[:, lanes] = (iota((256, 256), 0) == lane[:, lanes]).astype(F32).astype(BF16)
 
-    cell_rank = iota((128, 1), 0)
-    cell_id = (gx * 8 + lax.shift_right_logical(cell_rank, 4)) * 1024 + yz * 16 + lax.bitwise_and(cell_rank, 15)
-    found = jnp.zeros((128, 128), F32)
-    for tile in range(32):
-        label = (iota((1, 128), 1) + (tile * 128 + 1)).astype(F32)
-        found = found + jnp.where(cell[:, tile * 128 : tile * 128 + 128] == cell_id, label, 0.0)
-    owner = jnp.sum(found, axis=1, keepdims=True).astype(jnp.int32) - 1
-    owner_row = lax.shift_right_arithmetic(owner, 7)
-    owner_lane = lax.bitwise_and(owner, 127)
-    pick_row = (lax.bitwise_and(iota((128, 64), 1), 31) == owner_row).astype(F32).astype(BF16)
-
     def project(cells, rows):
         part = lax.dot_general(weights_z, cells, (((1,), (1,)), ((), ())), precision=HIGH, preferred_element_type=F32)
         return jnp.dot(part, rows, precision=HIGH, preferred_element_type=F32)
@@ -494,6 +483,17 @@
     @pl.loop(0, 2)
     def _(side):
         update(1 + 7 * side)
+
+    cell_rank = iota((128, 1), 0)
+    cell_id = (gx * 8 + lax.shift_right_logical(cell_rank, 4)) * 1024 + yz * 16 + lax.bitwise_and(cell_rank, 15)
+    found = jnp.zeros((128, 128), F32)
+    for tile in range(32):
+        label = (iota((1, 128), 1) + (tile * 128 + 1)).astype(F32)
+        found = found + jnp.where(cell[:, tile * 128 : tile * 128 + 128] == cell_id, label, 0.0)
+    owner = jnp.sum(found, axis=1, keepdims=True).astype(jnp.int32) - 1
+    owner_row = lax.shift_right_arithmetic(owner, 7)
+    owner_lane = lax.bitwise_and(owner, 127)
+    pick_row = (lax.bitwise_and(iota((128, 64), 1), 31) == owner_row).astype(F32).astype(BF16)
 
     @pl.when(follows)
     def _():

time: 38.2 us -> 38.1 us (level)
  no operation moved by 1% of the time
where the time goes in v8:
time: 38.1 us; the launch traced here: 38 us
  Pallas kernels  37.4 us (98%)
  between operations  0.64 us (2%)
    pallas_call x1, Pallas kernels, on_device(): pl.pallas_call(kernel, out_shape=(jax.ShapeDtypeStruct(adjoint.shape, F32...  36.5 us
    pallas_call x1, Pallas kernels, on_device(): pl.pallas_call(store_results, out_shape=tuple((jax.ShapeDtypeStruct(a.sha...  0.91 us

profile of v8, /device:TPU:1, one launch (start us, length us, event | category | flops | bytes accessed | tf_op | source)
XLA Modules:
  0.0 38.0 jit_solution(1830601122140862819)
XLA Ops:
  0.6 36.5 %adjoint_step.1 = (f32[12,8,16,128]{3,2,1,0:T(8,128)S(1)}, f32[7,1,67]{2,1,0:T(1,128)S(1)}, f32[1,64]{1,0:T(1,128)S(1)}) custom-call(f32[12,8,16,128]{3,2,1,0:T(8,128)} %adjoint.1, f32[12,8,16,128]{3,2,1,0:T(8,128)} %forward.1, f32[7,1,67]{2,1,0:T(1,128)} %bitcast.8, s32[1,16]{1,0:T(1,128)} %bitcast.9, f32[1,16]{1,0:T(1,128)} %bitcast.10, ...), custom_call_target="tpu_custom_call" | custom-call | tf_op jit(solution)/shard_map/adjoint_step/pallas_call | solution.py:580
  37.1 0.9 %store_results.1 = (f32[12,8,16,128]{3,2,1,0:T(8,128)}, f32[7,1,67]{2,1,0:T(1,128)}, f32[1,64]{1,0:T(1,128)}) custom-call(f32[12,8,16,128]{3,2,1,0:T(8,128)S(1)} %get-tuple-element.9.refs_0_, f32[7,1,67]{2,1,0:T(1,128)S(1)} %get-tuple-element.10.refs_1_, f32[1,64]{1,0:T(1,128)S(1)} %get-tuple-element.11.refs_2_), custom_call_target="tpu_custom_call" | custom-call | tf_op jit(solution)/shard_map/store_results/pallas_call | solution.py:640
